TPU v7x, 32 devices: a whole 2x2x4 slice. The times are simulated.
32 devices in a mesh: grp: 1, seq: 16 (over z, y, x), head: 1, srv: 2 (over core).
Axes of the slice: x: 2, y: 2, z: 4, core: 2. Of those that a mesh axis runs over, the one named last changes fastest.
Arguments:
- tokens: bfloat16 [4096, 4096], P(('grp', 'seq', 'srv'), 'head'), may hold values from -6 to 6
- norm_gain: float32 [4096], replicated, may hold values from 0.5 to 12, as said below
- wq: bfloat16 [4096, 4096], P(('seq', 'srv'), 'head'), may hold values from -0.09375 to 0.09375
- wk: bfloat16 [4096, 1024], P(('seq', 'srv'), 'head'), may hold values from -0.09375 to 0.09375
- wv: bfloat16 [4096, 1024], P(('seq', 'srv'), 'head'), may hold values from -0.09375 to 0.09375
- wo: bfloat16 [4096, 4096], P('head', ('seq', 'srv')), may hold values from -0.09375 to 0.09375
- doc_ids: int32 [4096], P(('grp', 'seq', 'srv')), may hold values from 0 to 7, never falling along the last dimension, each value on 1 to 3072 neighbouring positions
Outputs:
- mixed: bfloat16 [4096, 4096], P(('grp', 'seq', 'srv'), 'head')
Inputs may be any that keep to these rules, and one draw needn't show every extreme that they name: `norm_gain`: the gain is positive.
All inputs are finite; a program needn't handle non-finite values.
Results may differ from a plain program's by a relative error of at most 0.015.
The roundings to bfloat16 on the way count: a program that leaves them out, or rounds other values in their place, can miss the bound.
Values may be sent and summed in bfloat16 or wider, within the bound.
A program may use at most 128 MiB of HBM per device.

v0:
```python
import math

import jax
import jax.numpy as jnp
from jax import lax
from jax.sharding import PartitionSpec as P

QUERY_HEADS = 32
KV_HEAD_COUNT = 8
HEAD_WIDTH = 128


def rope(field, positions):
    half = field.shape[-1] // 2
    freqs = 500000.0 ** (-(jnp.arange(half, dtype=jnp.float32) * 2.0 / field.shape[-1]))
    angles = positions.astype(jnp.float32)[:, None] * freqs[None, :]
    cosine = jnp.cos(angles)[:, None, :]
    sine = jnp.sin(angles)[:, None, :]
    first = field[..., :half]
    second = field[..., half:]
    return jnp.concatenate(
        [first * cosine - second * sine, second * cosine + first * sine], axis=-1
    )


def local(tokens, norm_gain, wq, wk, wv, wo, doc_ids):
    tok_rows = tokens.shape[0]
    head_size = HEAD_WIDTH
    kv_local = wk.shape[1] // head_size
    query_group = QUERY_HEADS // KV_HEAD_COUNT
    source = tokens.astype(jnp.float32)
    whole = lax.all_gather(tokens, "head", axis=1, tiled=True).astype(jnp.float32)
    mean_sq = jnp.mean(whole * whole, axis=1, keepdims=True)
    normed_input = (whole * lax.rsqrt(mean_sq + 1e-05) * norm_gain[None, :]).astype(jnp.bfloat16)
    query_acc = jnp.dot(
        normed_input,
        lax.all_gather(wq, ("seq", "srv"), axis=0, tiled=True),
        preferred_element_type=jnp.float32,
    )
    key_acc = jnp.dot(
        normed_input,
        lax.all_gather(wk, ("seq", "srv"), axis=0, tiled=True),
        preferred_element_type=jnp.float32,
    )
    value_acc = jnp.dot(
        normed_input,
        lax.all_gather(wv, ("seq", "srv"), axis=0, tiled=True),
        preferred_element_type=jnp.float32,
    )
    first_pos = lax.axis_index(("seq", "srv")) * tok_rows
    positions = first_pos + jnp.arange(tok_rows, dtype=jnp.int32)
    query_matrix = rope(query_acc.reshape(tok_rows, kv_local * query_group, head_size), positions)
    query_matrix = query_matrix.astype(jnp.bfloat16).reshape(
        tok_rows, kv_local, query_group, head_size
    )
    key_matrix = rope(key_acc.reshape(tok_rows, kv_local, head_size), positions).astype(
        jnp.bfloat16
    )
    key_matrix = key_matrix.reshape(tok_rows, kv_local * head_size)
    value_matrix = value_acc.astype(jnp.bfloat16)
    scale = 1.0 / head_size**0.5

    def attend_block(carry, key_rows, value_rows, doc_rows, key_pos):
        run_top, run_total, run_acc = carry
        key_heads = key_rows.reshape(key_rows.shape[0], kv_local, head_size)
        value_heads = value_rows.reshape(value_rows.shape[0], kv_local, head_size)
        scores = (
            jnp.einsum(
                "qcgd,kcd->qcgk", query_matrix, key_heads, preferred_element_type=jnp.float32
            )
            * scale
        )
        allowed = (
            (key_pos[None, :] <= positions[:, None])
            & (key_pos[None, :] >= 0)
            & (doc_rows[None, :] == doc_ids[:, None])
        )
        allowed = allowed[:, None, None, :]
        masked = jnp.where(allowed, scores, -1e30)
        new_top = jnp.maximum(run_top, jnp.max(masked, axis=3))
        expd = jnp.where(allowed, jnp.exp(masked - new_top[..., None]), 0.0)
        factor = jnp.exp(run_top - new_top)
        new_total = run_total * factor + jnp.sum(expd, axis=3)
        weights = expd.astype(jnp.bfloat16)
        update = jnp.einsum(
            "qcgk,kcd->qcgd", weights, value_heads, preferred_element_type=jnp.float32
        )
        return (new_top, new_total, run_acc * factor[..., None] + update)

    start_state = (
        jnp.full((tok_rows, kv_local, query_group), -1e30, jnp.float32),
        jnp.zeros((tok_rows, kv_local, query_group), jnp.float32),
        jnp.zeros((tok_rows, kv_local, query_group, head_size), jnp.float32),
    )
    key_piece = lax.all_gather(key_matrix, ("seq", "srv"), axis=0, tiled=True)
    value_piece = lax.all_gather(value_matrix, ("seq", "srv"), axis=0, tiled=True)
    doc_piece = lax.all_gather(doc_ids, ("seq", "srv"), axis=0, tiled=True)
    count = key_piece.shape[0]
    width = math.gcd(count, 512)

    def step(inner, index):
        offset = index * width
        key_rows = lax.dynamic_slice_in_dim(key_piece, offset, width, 0)
        value_rows = lax.dynamic_slice_in_dim(value_piece, offset, width, 0)
        doc_rows = lax.dynamic_slice_in_dim(doc_piece, offset, width, 0)
        key_pos = offset + jnp.arange(width, dtype=jnp.int32)
        return (attend_block(inner, key_rows, value_rows, doc_rows, key_pos), None)

    def run_all(inner):
        result, unused = lax.scan(step, inner, jnp.arange(count // width, dtype=jnp.int32))
        return result

    beyond = jnp.int32(0) > first_pos + tok_rows - 1
    before = doc_piece[count - 1] < doc_ids[0]
    final_top, final_total, final_acc = lax.cond(
        beyond | before, lambda inner: inner, run_all, start_state
    )
    attended = (final_acc / final_total[..., None]).astype(jnp.bfloat16)
    attended = attended.reshape(tok_rows, kv_local * query_group * head_size)
    terms = jnp.dot(
        attended,
        lax.all_gather(wo, ("seq", "srv"), axis=1, tiled=True),
        preferred_element_type=jnp.float32,
    )
    summed = lax.psum_scatter(
        terms.astype(jnp.bfloat16), "head", scatter_dimension=1, tiled=True
    ).astype(jnp.float32)
    return (source + summed).astype(jnp.bfloat16)


def solution(mesh):
    in_specs = (
        P(("grp", "seq", "srv"), "head"),
        P(),
        P(("seq", "srv"), "head"),
        P(("seq", "srv"), "head"),
        P(("seq", "srv"), "head"),
        P("head", ("seq", "srv")),
        P(("grp", "seq", "srv")),
    )
    out_specs = P(("grp", "seq", "srv"), "head")
    return jax.shard_map(local, mesh=mesh, in_specs=in_specs, out_specs=out_specs, check_vma=False)
```

profile of v0, /device:TPU:0, one launch (start us, length us, event | category | flops | bytes accessed | tf_op | source)
XLA Modules:
  0.0 752.3 jit_solution(5832325511100395149)
XLA Ops:
  6.5 0.7 all-gather.8.cloned.1.call-update
  7.3 0.7 all-gather.14.cloned.1.call-update
  8.1 0.7 all-gather.12.cloned.1.call-update
  9.5 81.0 %all-gather.8.cloned.1.call-done = bf16[4096,1024]{1,0:T(8,128)(2,1)} async-done(((bf16[128,1024]{1,0:T(8,128)(2,1)}), bf16[4096,1024]{1,0:T(8,128)(2,1)}) %all-gather.8.cloned.1.call-update) | async-done | bytes 8388624 | tf_op jit(solution)/shard_map/all_gather | solution.py:42
  90.4 4.7 convolution_bitcast_fusion.1
  95.6 0.9 copy.20
  96.6 72.7 %all-gather.14.cloned.1.call-done = bf16[4096,1024]{1,0:T(8,128)(2,1)} async-done(((bf16[128,1024]{1,0:T(8,128)(2,1)}), bf16[4096,1024]{1,0:T(8,128)(2,1)}) %all-gather.14.cloned.1.call-update) | async-done | bytes 8388624 | tf_op jit(solution)/shard_map/all_gather | solution.py:47
  169.3 5.4 convolution_convert_fusion.1
  175.4 39.4 %all-gather = s32[32,1,128]{2,1,0:T(1,128)S(1)} all-gather(s32[1,1,128]{2,1,0:T(1,128)S(1)} %bitcast.78), channel_id=1, replica_groups=mesh['grp'=1,'seq'=16,'head'=1,'srv'=2] {'seq','srv'}, dimensions={0}, use_global_device_ids=true | all-gather | bytes 16896 | tf_op jit(solution)/shard_map/all_gather | solution.py:97
  215.9 149.8 %all-gather.12.cloned.1.call-done = bf16[4096,4096]{1,0:T(8,128)(2,1)} async-done(((bf16[128,4096]{1,0:T(8,128)(2,1)}), bf16[4096,4096]{1,0:T(8,128)(2,1)}) %all-gather.12.cloned.1.call-update) | async-done | bytes 33554448 | tf_op jit(solution)/shard_map/all_gather | solution.py:37
  365.7 13.2 %convolution_bitcast_fusion = f32[16,8,32,128]{3,1,2,0:T(8,128)S(1)} fusion(bf16[4096,4096]{1,0:T(8,128)(2,1)} %all-gather.12.cloned.1.call-done, bf16[128,4096]{1,0:T(8,128)(2,1)S(1)} %copy-done, f32[4096]{0:T(1024)S(1)} %copy-done.2, f32[128]{0:T(128)S(1)} %add_rsqrt_fusion), kind=kOutput, calls=%fused_computation.34 | convolution fusion | flops 4297064448 | bytes 36717056 | tf_op jit(solution)/shard_map/dot_general | solution.py:35
  379.2 0.8 subtract_convert_fusion
  381.5 77.4 %all-gather.10.cloned.1.call-done = bf16[4096,1024]{0,1:T(8,128)(2,1)} async-done(((bf16[128,1024]{0,1:T(8,128)(2,1)}), bf16[4096,1024]{0,1:T(8,128)(2,1)}) %all-gather.10.cloned.1.call-update) | async-done | bytes 8388624 | tf_op jit(solution)/shard_map/all_gather | solution.py:95
  458.9 78.4 %all-gather.16.cloned.1.call-done = bf16[4096,1024]{1,0:T(8,128)(2,1)} async-done(((bf16[128,1024]{1,0:T(8,128)(2,1)}), bf16[4096,1024]{1,0:T(8,128)(2,1)}) %all-gather.16.cloned.1.call-update) | async-done | bytes 8388624 | tf_op jit(solution)/shard_map/all_gather | solution.py:96
  537.2 174.9 %conditional.1 = (f32[128,8,4]{0,2,1:T(4,128)S(1)}, f32[128,8,4,128]{0,3,2,1:T(8,128)}) conditional(s32[]{:T(128)} %convert_element_type.44, (s32[]{:T(128)}, s32[128]{0:T(128)S(1)}, s32[4096]{0:T(1024)S(1)}, s32[128]{0:T(128)S(1)}, bf16[4096,1024]{0,1:T(8,128)(2,1)}, /*index=5*/bf16[128,8,4,128]{3,0,2,1:T(8,128)(2,1)S(1)}, ...), branch_computations={%region_1.6_spmd, %region_6.7_spmd} | conditional | flops 1102861952 | bytes 39335320 | solution.py:115
  537.3 174.9 %while.14 = (s32[]{:T(128)}, f32[128,8,4]{0,2,1:T(4,128)S(1)}, f32[128,8,4]{0,2,1:T(4,128)S(1)}, f32[128,8,4,128]{0,3,2,1:T(8,128)}, s32[8]{0:T(128)S(1)}, /*ind...) while((s32[]{:T(128)}, f32[128,8,4]{0,2,1:T(4,128)S(1)}, ...), condition=%wide.region_5.5_spmd.clone, body=%wide.region_2.4_spmd.clone.sunk | while | flops 1102861824 | bytes 39334116 | solution.py:110
  537.3 0.6 dynamic_slice.25
  538.9 1.3 constant_dynamic-slice_fusion.4
  540.2 4.7 fusion.40
  544.9 4.7 fusion.41
  549.6 1.3 constant_dynamic-slice_fusion.5
  551.5 7.0 bitcast_add_fusion.2
  558.5 0.6 dynamic_slice.25
  560.1 1.3 constant_dynamic-slice_fusion.4
  561.4 4.7 fusion.40
  566.2 4.5 fusion.41
  570.7 1.3 constant_dynamic-slice_fusion.5
  572.6 7.8 %bitcast_add_fusion.2 = f32[128,8,4,128]{0,3,2,1:T(8,128)} fusion(f32[128,8,4,128]{0,3,2,1:T(8,128)} %get-tuple-element.272, bf16[512,8,128,1]{0,2,3,1:T(8,128)(2,1)S(1)} %bitcast.69, f32[8,512,128,4]{2,1,3,0:T(8,128)} %get-tuple-element.251, f32[128,8,4]{0,2,1:T(4,128)S(1)} %select_maximum_fusion.2, pred[128,512]{0,1:T(8,128)(4,1)S(1)} %compare_and_fusion.2, ...), kind=kOutput, calls=%fused_computation.7.clone.1 | convolution fusion | flops 548929536 | bytes 13729793 | tf_op jit(solution)/shard_map/cond/branch_0_fun/while/body/eval_jaxpr/qcgk,kcd->qcgd/dot_general | solution.py:85
  580.4 0.6 dynamic_slice.25
  582.0 1.3 constant_dynamic-slice_fusion.4
  583.3 4.7 fusion.40
  588.0 4.6 fusion.41
  592.7 1.3 constant_dynamic-slice_fusion.5
  594.6 7.6 %bitcast_add_fusion.2 = f32[128,8,4,128]{0,3,2,1:T(8,128)} fusion(f32[128,8,4,128]{0,3,2,1:T(8,128)} %get-tuple-element.272, bf16[512,8,128,1]{0,2,3,1:T(8,128)(2,1)S(1)} %bitcast.69, f32[8,512,128,4]{2,1,3,0:T(8,128)} %get-tuple-element.251, f32[128,8,4]{0,2,1:T(4,128)S(1)} %select_maximum_fusion.2, pred[128,512]{0,1:T(8,128)(4,1)S(1)} %compare_and_fusion.2, ...), kind=kOutput, calls=%fused_computation.7.clone.1 | convolution fusion | flops 548929536 | bytes 13729793 | tf_op jit(solution)/shard_map/cond/branch_0_fun/while/body/eval_jaxpr/qcgk,kcd->qcgd/dot_general | solution.py:85
  602.2 0.6 dynamic_slice.25
  603.8 1.3 constant_dynamic-slice_fusion.4
  605.1 4.7 fusion.40
  609.8 5.0 fusion.41
  614.9 1.3 constant_dynamic-slice_fusion.5
  616.7 7.6 %bitcast_add_fusion.2 = f32[128,8,4,128]{0,3,2,1:T(8,128)} fusion(f32[128,8,4,128]{0,3,2,1:T(8,128)} %get-tuple-element.272, bf16[512,8,128,1]{0,2,3,1:T(8,128)(2,1)S(1)} %bitcast.69, f32[8,512,128,4]{2,1,3,0:T(8,128)} %get-tuple-element.251, f32[128,8,4]{0,2,1:T(4,128)S(1)} %select_maximum_fusion.2, pred[128,512]{0,1:T(8,128)(4,1)S(1)} %compare_and_fusion.2, ...), kind=kOutput, calls=%fused_computation.7.clone.1 | convolution fusion | flops 548929536 | bytes 13729793 | tf_op jit(solution)/shard_map/cond/branch_0_fun/while/body/eval_jaxpr/qcgk,kcd->qcgd/dot_general | solution.py:85
  626.0 1.3 constant_dynamic-slice_fusion.4
  627.3 4.7 fusion.40
  632.0 4.6 fusion.41
  636.7 1.3 constant_dynamic-slice_fusion.5
  638.5 7.7 %bitcast_add_fusion.2 = f32[128,8,4,128]{0,3,2,1:T(8,128)} fusion(f32[128,8,4,128]{0,3,2,1:T(8,128)} %get-tuple-element.272, bf16[512,8,128,1]{0,2,3,1:T(8,128)(2,1)S(1)} %bitcast.69, f32[8,512,128,4]{2,1,3,0:T(8,128)} %get-tuple-element.251, f32[128,8,4]{0,2,1:T(4,128)S(1)} %select_maximum_fusion.2, pred[128,512]{0,1:T(8,128)(4,1)S(1)} %compare_and_fusion.2, ...), kind=kOutput, calls=%fused_computation.7.clone.1 | convolution fusion | flops 548929536 | bytes 13729793 | tf_op jit(solution)/shard_map/cond/branch_0_fun/while/body/eval_jaxpr/qcgk,kcd->qcgd/dot_general | solution.py:85
  647.9 1.3 constant_dynamic-slice_fusion.4
  649.2 4.7 fusion.40
  653.9 4.5 fusion.41
  658.5 1.3 constant_dynamic-slice_fusion.5
  660.3 7.7 %bitcast_add_fusion.2 = f32[128,8,4,128]{0,3,2,1:T(8,128)} fusion(f32[128,8,4,128]{0,3,2,1:T(8,128)} %get-tuple-element.272, bf16[512,8,128,1]{0,2,3,1:T(8,128)(2,1)S(1)} %bitcast.69, f32[8,512,128,4]{2,1,3,0:T(8,128)} %get-tuple-element.251, f32[128,8,4]{0,2,1:T(4,128)S(1)} %select_maximum_fusion.2, pred[128,512]{0,1:T(8,128)(4,1)S(1)} %compare_and_fusion.2, ...), kind=kOutput, calls=%fused_computation.7.clone.1 | convolution fusion | flops 548929536 | bytes 13729793 | tf_op jit(solution)/shard_map/cond/branch_0_fun/while/body/eval_jaxpr/qcgk,kcd->qcgd/dot_general | solution.py:85
  669.7 1.4 constant_dynamic-slice_fusion.4
  671.1 4.7 fusion.40
  675.8 4.5 fusion.41
  680.4 1.3 constant_dynamic-slice_fusion.5
  682.3 7.8 %bitcast_add_fusion.2 = f32[128,8,4,128]{0,3,2,1:T(8,128)} fusion(f32[128,8,4,128]{0,3,2,1:T(8,128)} %get-tuple-element.272, bf16[512,8,128,1]{0,2,3,1:T(8,128)(2,1)S(1)} %bitcast.69, f32[8,512,128,4]{2,1,3,0:T(8,128)} %get-tuple-element.251, f32[128,8,4]{0,2,1:T(4,128)S(1)} %select_maximum_fusion.2, pred[128,512]{0,1:T(8,128)(4,1)S(1)} %compare_and_fusion.2, ...), kind=kOutput, calls=%fused_computation.7.clone.1 | convolution fusion | flops 548929536 | bytes 13729793 | tf_op jit(solution)/shard_map/cond/branch_0_fun/while/body/eval_jaxpr/qcgk,kcd->qcgd/dot_general | solution.py:85
  690.1 0.6 dynamic_slice.25
  691.7 1.3 constant_dynamic-slice_fusion.4
  693.0 4.7 fusion.40
  697.7 4.5 fusion.41
  702.3 1.3 constant_dynamic-slice_fusion.5
  704.1 8.0 %bitcast_add_fusion.2 = f32[128,8,4,128]{0,3,2,1:T(8,128)} fusion(f32[128,8,4,128]{0,3,2,1:T(8,128)} %get-tuple-element.272, bf16[512,8,128,1]{0,2,3,1:T(8,128)(2,1)S(1)} %bitcast.69, f32[8,512,128,4]{2,1,3,0:T(8,128)} %get-tuple-element.251, f32[128,8,4]{0,2,1:T(4,128)S(1)} %select_maximum_fusion.2, pred[128,512]{0,1:T(8,128)(4,1)S(1)} %compare_and_fusion.2, ...), kind=kOutput, calls=%fused_computation.7.clone.1 | convolution fusion | flops 548929536 | bytes 13729793 | tf_op jit(solution)/shard_map/cond/branch_0_fun/while/body/eval_jaxpr/qcgk,kcd->qcgd/dot_general | solution.py:85
  712.1 1.9 divide_convert_fusion
  714.1 17.3 %all-gather.18.cloned.1.call-done = bf16[4096,4096]{1,0:T(8,128)(2,1)} async-done(((bf16[4096,128]{1,0:T(8,128)(2,1)}), bf16[4096,4096]{1,0:T(8,128)(2,1)}) %all-gather.18.cloned.1.call-update) | async-done | bytes 33554448 | tf_op jit(solution)/shard_map/all_gather | solution.py:122
  731.4 14.1 %fusion.14 = bf16[128,4096]{1,0:T(8,128)(2,1)} fusion(bf16[128,4096]{0,1:T(8,128)(2,1)S(1)} %bitcast.71, bf16[4096,4096]{1,0:T(8,128)(2,1)} %all-gather.18.cloned.1.call-done, bf16[128,4096]{1,0:T(8,128)(2,1)S(1)} %copy-done.1), kind=kOutput, calls=%fused_computation.25 | convolution fusion | flops 4297588736 | bytes 36700160 | tf_op jit(solution)/shard_map/dot_general | solution.py:120
  (103 shorter events, 13.6 us)
Async XLA Ops:
  6.5 2.3 copy-start
  6.5 83.9 %copy-start.2 = (f32[4096]{0:T(1024)S(1)}, f32[4096]{0:T(1024)}, u32[]{:S(2)}) copy-start(f32[4096]{0:T(1024)} %param.12) | copy-start | bytes 49156
  6.5 83.9 %all-gather.8.cloned.1.call-start = ((), (), s32[]{:S(2)}) async-start(), calls=%async_computation | async-start | bytes 8650752 | tf_op jit(solution)/shard_map/all_gather | solution.py:42
  7.3 162.1 %all-gather.14.cloned.1.call-start = ((), (), s32[]{:S(2)}) async-start(), calls=%async_computation.3 | async-start | bytes 8650752 | tf_op jit(solution)/shard_map/all_gather | solution.py:47
  8.0 357.7 %all-gather.12.cloned.1.call-start = ((), (), s32[]{:S(2)}) async-start(), calls=%async_computation.2 | async-start | bytes 34603008 | tf_op jit(solution)/shard_map/all_gather | solution.py:37
  8.7 450.1 %all-gather.10.cloned.1.call-start = ((), (), s32[]{:S(2)}) async-start(), calls=%async_computation.1 | async-start | bytes 8650752 | tf_op jit(solution)/shard_map/all_gather | solution.py:95
  96.6 78.8 %copy-start.3 = (s32[128]{0:T(128)S(1)}, s32[128]{0:T(128)}, u32[]{:S(2)}) copy-start(s32[128]{0:T(128)} %param.17) | copy-start | bytes 1540
  96.6 440.7 %all-gather.16.cloned.1.call-start = ((), (), s32[]{:S(2)}) async-start(), calls=%async_computation.4 | async-start | bytes 8650752 | tf_op jit(solution)/shard_map/all_gather | solution.py:96
  174.8 556.6 %all-gather.18.cloned.1.call-start = ((), (), s32[]{:S(2)}) async-start(), calls=%async_computation.5 | async-start | bytes 34603008 | tf_op jit(solution)/shard_map/all_gather | solution.py:122
  712.1 19.3 %copy-start.1 = (bf16[128,4096]{1,0:T(8,128)(2,1)S(1)}, bf16[128,4096]{1,0:T(8,128)(2,1)}, u32[]{:S(2)}) copy-start(bf16[128,4096]{1,0:T(8,128)(2,1)} %param.11) | copy-start | bytes 3145732
Sparse Core Ops, SparseCore 0:
  10.2 80.1 all-gather.7
  93.3 76.0 all-gather.13
  172.2 193.4 all-gather.11
  368.4 90.4 all-gather.9
  461.6 75.6 all-gather.15
  538.6 192.7 all-gather.17
where the time goes:
time: 753 us; the launch traced here: 752 us
  waiting for transfers between devices  479 us (64%)
  matrix products  136 us (18%)
  other arithmetic  44 us (6%)
  blocking collectives  39.4 us (5%)
  local copies, waits for them, and re-layouts  33.6 us (4%)
  between operations  14.2 us (2%)
    all_gather x1, waiting for transfers between devices, local(): lax.all_gather(wq, ('seq', 'srv'), axis=0, tiled=True)  150 us
    all_gather x1, waiting for transfers between devices, local(): lax.all_gather(wk, ('seq', 'srv'), axis=0, tiled=True)  81 us
    all_gather x1, waiting for transfers between devices, local(): lax.all_gather(value_matrix, ('seq', 'srv'), axis=0, tiled=True)  78.4 us
    all_gather x1, waiting for transfers between devices, local(): key_piece = lax.all_gather(key_matrix, ('seq', 'srv'), axis=0, tiled=True)  77.4 us
    all_gather x1, waiting for transfers between devices, local(): lax.all_gather(wv, ('seq', 'srv'), axis=0, tiled=True)  72.7 us
    dot_general x8, matrix products, attend_block(): jnp.einsum('qcgk,kcd->qcgd', weights, value_heads, preferred_element_type...  61.2 us
    all_gather x1, blocking collectives, local(): doc_piece = lax.all_gather(doc_ids, ('seq', 'srv'), axis=0, tiled=True)  39.4 us
    dot_general x8, matrix products, attend_block(): jnp.einsum('qcgd,kcd->qcgk', query_matrix, key_heads, preferred_element_t...  37.7 us
  transfers between devices with their start and end apart: 6, of which 6 were waited for; matrix products, arithmetic and copies ran while one was open for 27% of the time, Pallas kernels for 0%

commit v1 on v0

--- a/solution.py
+++ b/solution.py
@@ -1,8 +1,11 @@
+import functools
 import math
 
 import jax
 import jax.numpy as jnp
 from jax import lax
+from jax.experimental import pallas as pl
+from jax.experimental.pallas import tpu as pltpu
 from jax.sharding import PartitionSpec as P
 
 QUERY_HEADS = 32
@@ -128,7 +131,159 @@
     return (source + summed).astype(jnp.bfloat16)
 
 
+def attention_kernel(head_count, key_block, lo_ref, mid_ref, diag_ref, end_ref, first_ref,
+                     q_ref, kv_ref, start_ref, out_ref, acc_ref, top_ref, total_ref):
+    block = pl.program_id(0)
+    rows = q_ref.shape[0]
+    top_ref[...] = jnp.full_like(top_ref, -1e30)
+    total_ref[...] = jnp.zeros_like(total_ref)
+    acc_ref[...] = jnp.zeros_like(acc_ref)
+    factor_log2 = 1.4426950408889634 / HEAD_WIDTH**0.5
+    starts = start_ref[...]
+    query_pos = (
+        first_ref[0] + block * rows + lax.broadcasted_iota(jnp.int32, (rows, key_block), 0)
+    )
+
+    def visit(index, masked):
+        offset = pl.multiple_of(index * key_block, key_block)
+        keys = kv_ref[pl.ds(offset, key_block), :HEAD_WIDTH]
+        values = kv_ref[pl.ds(offset, key_block), HEAD_WIDTH:]
+        if masked:
+            key_pos = offset + lax.broadcasted_iota(jnp.int32, (rows, key_block), 1)
+            allowed = (key_pos <= query_pos) & (key_pos >= starts)
+        for head in range(head_count):
+            columns = slice(head * HEAD_WIDTH, (head + 1) * HEAD_WIDTH)
+            scores = lax.dot_general(
+                q_ref[:, columns], keys, (((1,), (1,)), ((), ())),
+                preferred_element_type=jnp.float32,
+            )
+            if masked:
+                scores = jnp.where(allowed, scores, -1e30)
+            old_top = top_ref[head]
+            new_top = jnp.maximum(old_top, jnp.max(scores, axis=1, keepdims=True))
+            expd = jnp.exp2((scores - new_top[:, :1]) * factor_log2)
+            factor = jnp.exp2((old_top - new_top) * factor_log2)
+            top_ref[head] = new_top
+            total_ref[head] = total_ref[head] * factor + jnp.sum(expd, axis=1, keepdims=True)
+            acc_ref[:, columns] = acc_ref[:, columns] * factor + jnp.dot(
+                expd.astype(jnp.bfloat16), values, preferred_element_type=jnp.float32
+            )
+
+    low, mid, diag, end = lo_ref[block], mid_ref[block], diag_ref[block], end_ref[block]
+
+    @pl.loop(low, mid)
+    def _(index):
+        visit(index, True)
+
+    @pl.loop(mid, diag)
+    def _(index):
+        visit(index, False)
+
+    @pl.loop(diag, end)
+    def _(index):
+        visit(index, True)
+
+    for head in range(head_count):
+        columns = slice(head * HEAD_WIDTH, (head + 1) * HEAD_WIDTH)
+        out_ref[:, columns] = (acc_ref[:, columns] / total_ref[head]).astype(jnp.bfloat16)
+
+
+def attend(queries, keys_values, starts, first, query_block, key_block):
+    tokens, width = queries.shape
+    blocks = tokens // query_block
+    head_count = width // HEAD_WIDTH
+    begins = starts.reshape(blocks, query_block)
+    query_first = first + jnp.arange(blocks, dtype=jnp.int32) * query_block
+    low = begins[:, 0] // key_block
+    diag = jnp.maximum(low, query_first // key_block)
+    mid = jnp.clip((begins[:, -1] + key_block - 1) // key_block, low, diag)
+    end = (query_first + query_block + key_block - 1) // key_block
+    spec = pltpu.PrefetchScalarGridSpec(
+        num_scalar_prefetch=5,
+        grid=(blocks,),
+        in_specs=[
+            pl.BlockSpec((query_block, width), lambda i, *_: (i, 0)),
+            pl.BlockSpec(keys_values.shape, lambda i, *_: (0, 0)),
+            pl.BlockSpec((query_block, 1), lambda i, *_: (i, 0)),
+        ],
+        out_specs=pl.BlockSpec((query_block, width), lambda i, *_: (i, 0)),
+        scratch_shapes=[
+            pltpu.VMEM((query_block, width), jnp.float32),
+            pltpu.VMEM((head_count, query_block, HEAD_WIDTH), jnp.float32),
+            pltpu.VMEM((head_count, query_block, HEAD_WIDTH), jnp.float32),
+        ],
+    )
+    pairs = tokens * keys_values.shape[0] * head_count // 2
+    return pl.pallas_call(
+        functools.partial(attention_kernel, head_count, key_block),
+        out_shape=jax.ShapeDtypeStruct((tokens, width), jnp.bfloat16),
+        grid_spec=spec,
+        compiler_params=pltpu.CompilerParams(vmem_limit_bytes=48 * 1024 * 1024),
+        cost_estimate=pl.CostEstimate(
+            flops=4 * pairs * HEAD_WIDTH, bytes_accessed=8 << 20, transcendentals=pairs
+        ),
+    )(low, mid, diag, end, jnp.reshape(first, (1,)), queries, keys_values, starts[:, None])
+
+
+def plane_local(tokens, norm_gain, wq, wk, wv, wo, doc_ids):
+    tok_rows, model_width = tokens.shape
+    plane = lax.axis_size("h")
+    planes = lax.axis_size("z")
+    first_pos = lax.axis_index("z") * (tok_rows * plane)
+    source = tokens.astype(jnp.float32)
+    mean_sq = jnp.mean(source * source, axis=1, keepdims=True)
+    normed = (source * lax.rsqrt(mean_sq + 1e-05) * norm_gain[None, :]).astype(jnp.bfloat16)
+
+    wkv = jnp.concatenate(
+        [wk.reshape(-1, plane, HEAD_WIDTH), wv.reshape(-1, plane, HEAD_WIDTH)], axis=2
+    ).reshape(wk.shape[0], -1)
+    wkv_mine = lax.all_to_all(wkv, "h", 1, 0, tiled=True)
+    wq_mine = lax.all_to_all(wq, "h", 1, 0, tiled=True)
+    normed_all = lax.all_gather(normed, "h", axis=0, tiled=True)
+    wkv_all = lax.all_gather(wkv_mine, "z", axis=0, tiled=True)
+    wq_all = lax.all_gather(wq_mine, "z", axis=0, tiled=True)
+    doc_plane = lax.all_gather(doc_ids, "h", axis=0, tiled=True)
+    doc_all = lax.all_gather(doc_plane, "z", axis=0, tiled=True)
+
+    plane_rows = tok_rows * plane
+    positions = first_pos + jnp.arange(plane_rows, dtype=jnp.int32)
+    doc_mine = doc_plane
+    starts = jnp.sum((doc_all[None, :] < doc_mine[:, None]).astype(jnp.int32), axis=1)
+
+    kv_acc = jnp.dot(normed_all, wkv_all, preferred_element_type=jnp.float32)
+    keys = rope(kv_acc[:, None, :HEAD_WIDTH], positions)[:, 0]
+    kv_mine = jnp.concatenate([keys, kv_acc[:, HEAD_WIDTH:]], axis=1).astype(jnp.bfloat16)
+    kv_all = lax.all_gather(kv_mine, "z", axis=0, tiled=True)
+
+    query_acc = jnp.dot(normed_all, wq_all, preferred_element_type=jnp.float32)
+    queries = rope(query_acc.reshape(plane_rows, -1, HEAD_WIDTH), positions)
+    queries = queries.astype(jnp.bfloat16).reshape(plane_rows, -1)
+
+    wo_all = lax.all_gather(wo, "z", axis=1, tiled=True)
+    attended = attend(queries, kv_all, starts, first_pos, 256, 512)
+    attended_all = lax.all_gather(attended, "h", axis=1, tiled=True)
+    terms = jnp.dot(attended_all, wo_all, preferred_element_type=jnp.float32).astype(jnp.bfloat16)
+    rows_mine = lax.all_to_all(terms, "h", 0, 1, tiled=True)
+    summed = rows_mine.reshape(tok_rows, plane, planes, -1).transpose(0, 2, 1, 3)
+    summed = summed.reshape(tok_rows, model_width).astype(jnp.float32)
+    return (source + summed).astype(jnp.bfloat16)
+
+
+def plane_solution(mesh, planes):
+    folded = jax.sharding.Mesh(mesh.devices.reshape(planes, KV_HEAD_COUNT), ("z", "h"))
+    rows = P(("z", "h"))
+    return jax.shard_map(
+        plane_local,
+        mesh=folded,
+        in_specs=(rows, P(), rows, rows, rows, P(None, ("z", "h")), rows),
+        out_specs=rows,
+        check_vma=False,
+    )
+
+
 def solution(mesh):
+    if mesh.shape["grp"] == 1 and mesh.shape["head"] == 1 and mesh.size % KV_HEAD_COUNT == 0:
+        return plane_solution(mesh, mesh.size // KV_HEAD_COUNT)
     in_specs = (
         P(("grp", "seq", "srv"), "head"),
         P(),

time: 753 us -> 432 us (0.57)
  waiting for transfers between devices: 479 us -> 272 us
  matrix products: 136 us -> 23.6 us
  blocking collectives: 39.4 us -> 73.6 us
  other arithmetic: 44 us -> 16.9 us
  local copies, waits for them, and re-layouts: 33.6 us -> 17.7 us
  Pallas kernels: 0 us -> 13.6 us
    all_gather x6, waiting for transfers between devices: 477 us -> 271 us  [the longest x1 65.4 us: plane_local(): wo_all = lax.all_gather(wo, 'z', axis=1, tiled=True)]
    dot_general x20 -> x3, matrix products: 136 us -> 23.6 us  [the longest x1 9.05 us: plane_local(): jnp.dot(attended_all, wo_all, preferred_element_type=jnp.float32)]
    all_to_all x0 -> x3, blocking collectives: none -> 50.4 us  [the longest x1 17.9 us: plane_local(): rows_mine = lax.all_to_all(terms, 'h', 0, 1, tiled=True)]
    reduce_sum x9 -> x2, other arithmetic: 37.3 us -> 2.05 us  [the longest x1 1.77 us: plane_local(): jnp.sum((doc_all[None, :] < doc_mine[:, None]).astype(jnp.int32), axis=1)]
    dynamic_slice x40 -> x0, local copies, waits for them, and re-layouts: 30.9 us -> none  [the longest x16 14.8 us: step(): value_rows = lax.dynamic_slice_in_dim(value_piece, offset, width, 0)]
    all_gather x1 -> x2, blocking collectives: 39.4 us -> 23.2 us  [the longest x1 14.5 us: plane_local(): doc_all = lax.all_gather(doc_plane, 'z', axis=0, tiled=True)]
    pallas_call x0 -> x1, Pallas kernels: none -> 13.6 us  [attend(): pl.pallas_call(functools.partial(attention_kernel, head_count, key_block)...]
    unnamed x10 -> x16, local copies, waits for them, and re-layouts: 0.48 us -> 9.27 us
  transfers between devices with their start and end apart: 6 -> 6, of which waited for: 6 -> 6; matrix products, arithmetic and copies ran while one was open for 27% -> 9% of each run, Pallas kernels for 0% -> 3%
where the time goes in v1:
time: 432 us; the launch traced here: 431 us
  waiting for transfers between devices  272 us (63%)
  blocking collectives  73.6 us (17%)
  matrix products  23.6 us (5%)
  local copies, waits for them, and re-layouts  17.7 us (4%)
  other arithmetic  16.9 us (4%)
  between operations  13.7 us (3%)
  Pallas kernels  13.6 us (3%)
    all_gather x1, waiting for transfers between devices, plane_local(): wo_all = lax.all_gather(wo, 'z', axis=1, tiled=True)  65.4 us
    all_gather x1, waiting for transfers between devices, plane_local(): attended_all = lax.all_gather(attended, 'h', axis=1, tiled=True)  55.9 us
    all_gather x1, waiting for transfers between devices, plane_local(): normed_all = lax.all_gather(normed, 'h', axis=0, tiled=True)  55 us
    all_gather x1, waiting for transfers between devices, plane_local(): wq_all = lax.all_gather(wq_mine, 'z', axis=0, tiled=True)  43.5 us
    all_gather x1, waiting for transfers between devices, plane_local(): kv_all = lax.all_gather(kv_mine, 'z', axis=0, tiled=True)  27.5 us
    all_gather x1, waiting for transfers between devices, plane_local(): wkv_all = lax.all_gather(wkv_mine, 'z', axis=0, tiled=True)  23.8 us
    all_to_all x1, blocking collectives, plane_local(): rows_mine = lax.all_to_all(terms, 'h', 0, 1, tiled=True)  17.9 us
    all_to_all x1, blocking collectives, plane_local(): wq_mine = lax.all_to_all(wq, 'h', 1, 0, tiled=True)  17.8 us
  transfers between devices with their start and end apart: 6, of which 6 were waited for; matrix products, arithmetic and copies ran while one was open for 9% of the time, Pallas kernels for 3%

profile of v1, /device:TPU:0, one launch (start us, length us, event | category | flops | bytes accessed | tf_op | source)
XLA Modules:
  0.0 431.1 jit_solution(7550992423009109318)
XLA Ops:
  6.5 0.0 all-gather.12.cloned.1.call-start
  6.5 1.1 copy.56
  7.7 0.0 copy-start.1
  7.7 1.2 copy.57
  8.9 0.0 copy-start.3
  8.9 14.7 %all_to_all.48 = bf16[128,8,256]{0,2,1:T(8,128)(2,1)S(1)} all-to-all(bf16[128,8,256]{0,2,1:T(8,128)(2,1)S(1)} %pad_maximum_fusion.1), channel_id=1, replica_groups=mesh['grp'=1,'seq'=16,'head'=1,'srv'=2] {'seq':(4)4,'srv'}, dimensions={1} | all-to-all | bytes 1048576 | tf_op jit(solution)/shard_map/all_to_all | solution.py:240
  23.7 1.0 copy.58
  24.7 0.0 all-gather.12.cloned.1.call-update
  24.7 0.0 copy-start.2
  24.7 0.0 all-gather.8.cloned.1.call-start
  24.8 0.0 copy-done.1
  24.8 0.3 fusion
  25.1 0.0 copy-done.3
  25.1 1.3 fusion.2
  26.4 0.0 all-gather.8.cloned.1.call-update
  26.4 0.0 all-gather.10.cloned.1.call-start
  26.4 0.0 copy-done.2
  26.5 0.7 copy.52
  27.1 17.8 %all_to_all.49 = bf16[128,8,512]{0,2,1:T(8,128)(2,1)S(1)} all-to-all(bf16[128,8,512]{0,2,1:T(8,128)(2,1)S(1)} %bitcast.41), channel_id=1, replica_groups=mesh['grp'=1,'seq'=16,'head'=1,'srv'=2] {'seq':(4)4,'srv'}, dimensions={1} | all-to-all | bytes 2097152 | tf_op jit(solution)/shard_map/all_to_all | solution.py:241
  44.9 1.3 copy.53
  46.2 0.0 all-gather.10.cloned.1.call-update
  46.3 0.0 all-gather.14.cloned.1.call-start
  46.3 23.8 %all-gather.12.cloned.1.call-done = bf16[4096,256]{1,0:T(8,128)(2,1)} async-done(((bf16[1024,256]{1,0:T(8,128)(2,1)}), bf16[4096,256]{1,0:T(8,128)(2,1)}) %all-gather.12.cloned.1.call-update) | async-done | bytes 2097168 | tf_op jit(solution)/shard_map/all_gather | solution.py:243
  70.1 55.0 %all-gather.8.cloned.1.call-done = bf16[1024,4096]{1,0:T(8,128)(2,1)} async-done(((bf16[128,4096]{1,0:T(8,128)(2,1)}), bf16[1024,4096]{1,0:T(8,128)(2,1)}) %all-gather.8.cloned.1.call-update) | async-done | bytes 8388624 | tf_op jit(solution)/shard_map/all_gather | solution.py:242
  125.2 6.3 %fusion.17 = f32[1024,256]{1,0:T(8,128)S(1)} fusion(bf16[1024,4096]{1,0:T(8,128)(2,1)} %all-gather.8.cloned.1.call-done, bf16[4096,256]{1,0:T(8,128)(2,1)} %all-gather.12.cloned.1.call-done), kind=kOutput, calls=%fused_computation.58 | convolution fusion | flops 2147483648 | bytes 11534336 | tf_op jit(solution)/shard_map/dot_general | solution.py:253
  131.6 2.4 fusion.9
  134.0 0.0 copy-start.4
  134.0 0.1 maximum_bitcast_fusion
  134.2 0.9 pad_maximum_fusion.2
  135.0 0.0 all-gather.14.cloned.1.call-update
  135.1 0.0 all-gather.18.cloned.1.call-start
  135.1 0.5 all-gather.18.cloned.1.call-update
  135.7 0.0 all-gather.16.cloned.1.call-start
  135.7 0.0 copy-done.4
  135.7 8.7 %all-gather = s32[8,1,128]{2,1,0:T(1,128)S(1)} all-gather(s32[1,1,128]{2,1,0:T(1,128)S(1)} %bitcast.51), channel_id=1, replica_groups=mesh['grp'=1,'seq'=16,'head'=1,'srv'=2] {'seq':(4)4,'srv'}, dimensions={0}, use_global_device_ids=true | all-gather | bytes 4608 | tf_op jit(solution)/shard_map/all_gather | solution.py:245
  144.4 14.5 %all_gather.25 = s32[4096]{0:T(1024)S(1)} all-gather(s32[1024]{0:T(1024)S(1)} %bitcast.49), channel_id=1, replica_groups=mesh['grp'=1,'seq'=16,'head'=1,'srv'=2] {'seq':(1)4}, dimensions={0}, use_global_device_ids=true | all-gather | bytes 20480 | tf_op jit(solution)/shard_map/all_gather | solution.py:246
  158.9 1.8 convert_reduce_fusion
  160.7 0.2 copy.62.start_ref
  161.0 0.2 fusion.12
  161.2 3.1 multiply_cosine_fusion.1
  164.3 43.5 %all-gather.10.cloned.1.call-done = bf16[4096,512]{1,0:T(8,128)(2,1)} async-done(((bf16[1024,512]{1,0:T(8,128)(2,1)}), bf16[4096,512]{1,0:T(8,128)(2,1)}) %all-gather.10.cloned.1.call-update) | async-done | bytes 4194320 | tf_op jit(solution)/shard_map/all_gather | solution.py:244
  207.8 8.2 %fusion.16 = f32[1024,512]{0,1:T(8,128)S(1)} fusion(bf16[1024,4096]{1,0:T(8,128)(2,1)} %all-gather.8.cloned.1.call-done, bf16[4096,512]{1,0:T(8,128)(2,1)} %all-gather.10.cloned.1.call-done), kind=kOutput, calls=%fused_computation.57 | convolution fusion | flops 4294967296 | bytes 14680064 | tf_op jit(solution)/shard_map/dot_general | solution.py:258
  216.0 1.2 fusion.15
  217.2 2.7 copy.65
  220.0 1.8 copy.66
  221.7 2.9 subtract_convert_fusion
  224.6 1.4 pad_maximum_fusion
  226.0 0.2 copy.71
  226.2 27.5 %all-gather.14.cloned.1.call-done.kv_ref = bf16[4096,256]{1,0:T(8,128)(2,1)} async-done(((bf16[1024,256]{1,0:T(8,128)(2,1)}), bf16[4096,256]{1,0:T(8,128)(2,1)}) %all-gather.14.cloned.1.call-update) | async-done | bytes 2097168 | tf_op jit(solution)/shard_map/all_gather | solution.py:256
  253.7 0.0 copy-start
  253.7 1.6 copy-done
  255.3 13.6 %shard_map.73 = bf16[1024,512]{1,0:T(8,128)(2,1)} custom-call(s32[4]{0:T(128)S(1)} %get-tuple-element.9.lo_ref, s32[4]{0:T(128)S(1)} %get-tuple-element.7.mid_ref, s32[4]{0:T(128)S(1)} %get-tuple-element.8.diag_ref, s32[4]{0:T(128)S(1)} %get-tuple-element.18.end_ref, s32[1]{0:T(128)} %bitcast.2.first_ref, bf16[1024,512]{1,0:T(8,128)(2,1)S(1)} %bitcast.36, ...), custom_call_target="tpu_custom_call" | custom-call | flops 4294967296 | bytes 8388608 | tf_op jit(solution)/shard_map/pallas_call | solution.py:217
  268.9 0.0 all-gather.16.cloned.1.call-update
  268.9 65.4 %all-gather.18.cloned.1.call-done = bf16[4096,512]{1,0:T(8,128)(2,1)} async-done(((bf16[4096,128]{1,0:T(8,128)(2,1)}), bf16[4096,512]{1,0:T(8,128)(2,1)}) %all-gather.18.cloned.1.call-update) | async-done | bytes 4194320 | tf_op jit(solution)/shard_map/all_gather | solution.py:262
  334.4 55.9 %all-gather.16.cloned.1.call-done = bf16[1024,4096]{1,0:T(8,128)(2,1)} async-done(((bf16[1024,512]{1,0:T(8,128)(2,1)}), bf16[1024,4096]{1,0:T(8,128)(2,1)}) %all-gather.16.cloned.1.call-update) | async-done | bytes 8388624 | tf_op jit(solution)/shard_map/all_gather | solution.py:264
  390.2 9.1 %convolution_convert_fusion = bf16[1024,512]{1,0:T(8,128)(2,1)S(1)} fusion(bf16[1024,4096]{1,0:T(8,128)(2,1)} %all-gather.16.cloned.1.call-done, bf16[4096,512]{1,0:T(8,128)(2,1)} %all-gather.18.cloned.1.call-done), kind=kOutput, calls=%fused_computation.11 | convolution fusion | flops 4295491584 | bytes 13631488 | tf_op jit(solution)/shard_map/dot_general | solution.py:265
  399.3 17.9 %all_to_all.50 = bf16[8,128,512]{2,1,0:T(8,128)(2,1)S(1)} all-to-all(bf16[8,128,512]{2,1,0:T(8,128)(2,1)S(1)} %bitcast.45), channel_id=1, replica_groups=mesh['grp'=1,'seq'=16,'head'=1,'srv'=2] {'seq':(4)4,'srv'}, dimensions={0} | all-to-all | bytes 2097152 | tf_op jit(solution)/shard_map/all_to_all | solution.py:266
  417.2 0.3 convert_bitcast_fusion
  417.5 1.8 reshape.159
  419.2 2.8 copy.63
  422.1 2.2 fusion.3
  (8 shorter events, 0.2 us)
Async XLA Ops:
  6.5 63.6 %all-gather.12.cloned.1.call-start = ((), (), s32[]{:S(2)}) async-start(), calls=%async_computation.5 | async-start | bytes 2621440 | tf_op jit(solution)/shard_map/all_gather | solution.py:243
  7.7 17.1 %copy-start.1 = (bf16[128,4096]{1,0:T(8,128)(2,1)S(1)}, bf16[128,4096]{1,0:T(8,128)(2,1)}, u32[]{:S(2)}) copy-start(bf16[128,4096]{1,0:T(8,128)(2,1)} %param.7) | copy-start | bytes 3145732
  8.9 16.1 %copy-start.3 = (f32[4096]{0:T(1024)S(1)}, f32[4096]{0:T(1024)}, u32[]{:S(2)}) copy-start(f32[4096]{0:T(1024)} %param.8) | copy-start | bytes 49156
  24.7 1.8 copy-start.2
  24.7 100.5 %all-gather.8.cloned.1.call-start = ((), (), s32[]{:S(2)}) async-start(), calls=%async_computation.3 | async-start | bytes 9437184 | tf_op jit(solution)/shard_map/all_gather | solution.py:242
  26.4 181.4 %all-gather.10.cloned.1.call-start = ((), (), s32[]{:S(2)}) async-start(), calls=%async_computation.4 | async-start | bytes 5242880 | tf_op jit(solution)/shard_map/all_gather | solution.py:244
  46.3 207.5 %all-gather.14.cloned.1.call-start = ((), (), s32[]{:S(2)}) async-start(), calls=%async_computation.6 | async-start | bytes 2621440 | tf_op jit(solution)/shard_map/all_gather | solution.py:256
  134.0 1.7 copy-start.4
  135.1 199.3 %all-gather.18.cloned.1.call-start = ((), (), s32[]{:S(2)}) async-start(), calls=%async_computation.8 | async-start | bytes 5242880 | tf_op jit(solution)/shard_map/all_gather | solution.py:262
  135.7 254.6 %all-gather.16.cloned.1.call-start = ((), (), s32[]{:S(2)}) async-start(), calls=%async_computation.7 | async-start | bytes 9437184 | tf_op jit(solution)/shard_map/all_gather | solution.py:264
  253.7 1.6 copy-start
Sparse Core Ops, SparseCore 0:
  24.8 45.2 all-gather.11
  72.0 53.1 all-gather.7
  126.8 80.9 all-gather.9
  209.2 44.4 all-gather.13
  255.1 79.1 all-gather.17
  336.1 54.1 all-gather.15

commit v2 on v1

--- a/solution.py
+++ b/solution.py
@@ -220,7 +220,7 @@
         grid_spec=spec,
         compiler_params=pltpu.CompilerParams(vmem_limit_bytes=48 * 1024 * 1024),
         cost_estimate=pl.CostEstimate(
-            flops=4 * pairs * HEAD_WIDTH, bytes_accessed=8 << 20, transcendentals=pairs
+            flops=32 * pairs * HEAD_WIDTH, bytes_accessed=128 << 20, transcendentals=pairs
         ),
     )(low, mid, diag, end, jnp.reshape(first, (1,)), queries, keys_values, starts[:, None])
 
@@ -234,33 +234,44 @@
     mean_sq = jnp.mean(source * source, axis=1, keepdims=True)
     normed = (source * lax.rsqrt(mean_sq + 1e-05) * norm_gain[None, :]).astype(jnp.bfloat16)
 
-    wkv = jnp.concatenate(
-        [wk.reshape(-1, plane, HEAD_WIDTH), wv.reshape(-1, plane, HEAD_WIDTH)], axis=2
-    ).reshape(wk.shape[0], -1)
-    wkv_mine = lax.all_to_all(wkv, "h", 1, 0, tiled=True)
-    wq_mine = lax.all_to_all(wq, "h", 1, 0, tiled=True)
+    width = wq.shape[1] // plane
+    pack = 16
+    pieces = [weight.reshape(tok_rows, plane, -1) for weight in (wq, wk, wv)]
+    weights = jnp.concatenate(pieces, axis=2)
+    doc_rows = jnp.zeros((pack, plane, weights.shape[2]), jnp.bfloat16)
+    doc_rows = doc_rows.at[0, :, :tok_rows].set(doc_ids.astype(jnp.bfloat16))
+    sent = jnp.concatenate([weights, doc_rows], axis=0)
+    sent, normed = lax.optimization_barrier((sent, normed))
     normed_all = lax.all_gather(normed, "h", axis=0, tiled=True)
-    wkv_all = lax.all_gather(wkv_mine, "z", axis=0, tiled=True)
-    wq_all = lax.all_gather(wq_mine, "z", axis=0, tiled=True)
-    doc_plane = lax.all_gather(doc_ids, "h", axis=0, tiled=True)
-    doc_all = lax.all_gather(doc_plane, "z", axis=0, tiled=True)
+    landed = lax.all_to_all(sent.reshape(tok_rows + pack, -1), "h", 1, 0, tiled=True)
+    landed = landed.reshape(plane, tok_rows + pack, -1)
+    doc_plane = landed[:, tok_rows, :tok_rows].reshape(-1)
+    w_mine = landed[:, :tok_rows].reshape(plane * tok_rows, -1)
+    w_mine, normed_all = lax.optimization_barrier((w_mine, normed_all))
+    w_all = lax.all_gather(w_mine, "z", axis=0, tiled=True)
 
     plane_rows = tok_rows * plane
     positions = first_pos + jnp.arange(plane_rows, dtype=jnp.int32)
+
+    kv_acc = jnp.dot(normed_all, w_all[:, width:], preferred_element_type=jnp.float32)
+    keys = rope(kv_acc[:, None, :HEAD_WIDTH], positions)[:, 0]
+    kv_mine = jnp.concatenate([keys, kv_acc[:, HEAD_WIDTH:]], axis=1).astype(jnp.bfloat16)
+    doc_fold = doc_plane.reshape(-1, 2 * HEAD_WIDTH)
+    doc_fold = jnp.pad(doc_fold, ((0, -doc_fold.shape[0] % pack), (0, 0)))
+    kv_docs = lax.all_gather(jnp.concatenate([kv_mine, doc_fold], axis=0), "z", axis=0)
+    kv_all = kv_docs[:, :plane_rows].reshape(planes * plane_rows, -1)
+    doc_all = kv_docs[:, plane_rows:].reshape(planes, -1)[:, :plane_rows].reshape(-1)
     doc_mine = doc_plane
     starts = jnp.sum((doc_all[None, :] < doc_mine[:, None]).astype(jnp.int32), axis=1)
 
-    kv_acc = jnp.dot(normed_all, wkv_all, preferred_element_type=jnp.float32)
-    keys = rope(kv_acc[:, None, :HEAD_WIDTH], positions)[:, 0]
-    kv_mine = jnp.concatenate([keys, kv_acc[:, HEAD_WIDTH:]], axis=1).astype(jnp.bfloat16)
-    kv_all = lax.all_gather(kv_mine, "z", axis=0, tiled=True)
-
-    query_acc = jnp.dot(normed_all, wq_all, preferred_element_type=jnp.float32)
+    query_acc = jnp.dot(normed_all, w_all[:, :width], preferred_element_type=jnp.float32)
     queries = rope(query_acc.reshape(plane_rows, -1, HEAD_WIDTH), positions)
     queries = queries.astype(jnp.bfloat16).reshape(plane_rows, -1)
 
+    wo, kv_all = lax.optimization_barrier((wo, kv_all))
     wo_all = lax.all_gather(wo, "z", axis=1, tiled=True)
     attended = attend(queries, kv_all, starts, first_pos, 256, 512)
+    attended, wo_all = lax.optimization_barrier((attended, wo_all))
     attended_all = lax.all_gather(attended, "h", axis=1, tiled=True)
     terms = jnp.dot(attended_all, wo_all, preferred_element_type=jnp.float32).astype(jnp.bfloat16)
     rows_mine = lax.all_to_all(terms, "h", 0, 1, tiled=True)

time: 432 us -> 437 us (1.012)
  blocking collectives: 73.6 us -> 57.4 us
  waiting for transfers between devices: 272 us -> 286 us
  local copies, waits for them, and re-layouts: 17.7 us -> 24.8 us
    all_gather x3 -> x2, waiting for transfers between devices: 94.8 us -> 158 us  [the longest x1 117 us: plane_local(): w_all = lax.all_gather(w_mine, 'z', axis=0, tiled=True)]
    all_gather x1, waiting for transfers between devices: 55 us -> 30.2 us  [plane_local(): normed_all = lax.all_gather(normed, 'h', axis=0, tiled=True)]
    all_gather x1, waiting for transfers between devices: 65.4 us -> 41.6 us  [plane_local(): wo_all = lax.all_gather(wo, 'z', axis=1, tiled=True)]
    all_gather x2 -> x0, blocking collectives: 23.2 us -> none  [the longest x1 14.5 us: plane_local(): doc_all = lax.all_gather(doc_plane, 'z', axis=0, tiled=True)]
    all_to_all x2 -> x1, blocking collectives: 32.5 us -> 39.5 us  [plane_local(): lax.all_to_all(sent.reshape(tok_rows + pack, -1), 'h', 1, 0, tiled=True)]
    unnamed x16 -> x25, local copies, waits for them, and re-layouts: 9.27 us -> 10.9 us
  transfers between devices with their start and end apart: 6 -> 5, of which waited for: 6 -> 5; matrix products, arithmetic and copies ran while one was open for 9% -> 7% of each run, Pallas kernels for 3% -> 3%
where the time goes in v2:
time: 437 us; the launch traced here: 436 us
  waiting for transfers between devices  286 us (65%)
  blocking collectives  57.4 us (13%)
  local copies, waits for them, and re-layouts  24.8 us (6%)
  matrix products  23.6 us (5%)
  other arithmetic  17.4 us (4%)
  between operations  13.4 us (3%)
  Pallas kernels  13.1 us (3%)
    all_gather x1, waiting for transfers between devices, plane_local(): w_all = lax.all_gather(w_mine, 'z', axis=0, tiled=True)  117 us
    all_gather x1, waiting for transfers between devices, plane_local(): attended_all = lax.all_gather(attended, 'h', axis=1, tiled=True)  55.9 us
    all_gather x1, waiting for transfers between devices, plane_local(): lax.all_gather(jnp.concatenate([kv_mine, doc_fold], axis=0), 'z', axis=0)  41.8 us
    all_gather x1, waiting for transfers between devices, plane_local(): wo_all = lax.all_gather(wo, 'z', axis=1, tiled=True)  41.6 us
    all_to_all x1, blocking collectives, plane_local(): lax.all_to_all(sent.reshape(tok_rows + pack, -1), 'h', 1, 0, tiled=True)  39.5 us
    all_gather x1, waiting for transfers between devices, plane_local(): normed_all = lax.all_gather(normed, 'h', axis=0, tiled=True)  30.2 us
    all_to_all x1, blocking collectives, plane_local(): rows_mine = lax.all_to_all(terms, 'h', 0, 1, tiled=True)  17.9 us
    pallas_call x1, Pallas kernels, attend(): pl.pallas_call(functools.partial(attention_kernel, head_count, key_block)...  13.1 us
  transfers between devices with their start and end apart: 5, of which 5 were waited for; matrix products, arithmetic and copies ran while one was open for 7% of the time, Pallas kernels for 3%

profile of v2, /device:TPU:0, one launch (start us, length us, event | category | flops | bytes accessed | tf_op | source)
XLA Modules:
  0.0 436.3 jit_solution(2118729105223750101)
XLA Ops:
  6.5 0.0 copy-start.4
  6.5 0.0 copy-start.5
  6.5 0.0 copy-start.2
  6.5 0.0 all-gather.7.cloned.1.call-start
  6.5 0.8 convert_bitcast_fusion.1
  7.3 0.1 copy.53
  7.5 0.0 copy-start.6
  7.5 2.3 copy.40
  9.7 0.0 copy-done.4
  9.7 0.2 copy.41
  9.9 0.0 copy-done.5
  9.9 0.8 copy.42
  10.8 0.0 copy-done.2
  10.8 0.3 fusion.2
  11.1 0.0 copy-done.6
  11.1 1.3 fusion.4
  12.4 0.2 scatter.8
  12.6 1.8 pad_maximum_fusion
  14.4 0.0 all-gather.7.cloned.1.call-update
  14.4 0.0 all-gather.9.cloned.1.call-start
  14.5 2.5 copy.44
  17.0 39.5 %all_to_all.26 = bf16[144,8,768]{2,0,1:T(8,128)(2,1)S(1)} all-to-all(bf16[144,8,768]{2,0,1:T(8,128)(2,1)} %copy.44), channel_id=1, replica_groups=mesh['grp'=1,'seq'=16,'head'=1,'srv'=2] {'seq':(4)4,'srv'}, dimensions={1} | all-to-all | bytes 3538944 | tf_op jit(solution)/shard_map/all_to_all | solution.py:246
  56.4 1.3 slice.84
  57.7 30.2 %all-gather.7.cloned.1.call-done = bf16[1024,4096]{1,0:T(8,128)(2,1)} async-done(((bf16[128,4096]{1,0:T(8,128)(2,1)}), bf16[1024,4096]{1,0:T(8,128)(2,1)}) %all-gather.7.cloned.1.call-update) | async-done | bytes 8388624 | tf_op jit(solution)/shard_map/all_gather | solution.py:245
  87.9 0.0 all-gather.9.cloned.1.call-update
  88.0 0.0 all-gather.15.cloned.1.call-start
  88.1 0.1 copy.45
  88.2 116.7 %all-gather.9.cloned.1.call-done = bf16[4096,768]{1,0:T(8,128)(2,1)} async-done(((bf16[1024,768]{1,0:T(8,128)(2,1)}), bf16[4096,768]{1,0:T(8,128)(2,1)}) %all-gather.9.cloned.1.call-update) | async-done | bytes 6291472 | tf_op jit(solution)/shard_map/all_gather | solution.py:251
  204.9 6.3 %fusion.6 = f32[1024,256]{0,1:T(8,128)S(1)} fusion(bf16[1024,4096]{1,0:T(8,128)(2,1)} %all-gather.7.cloned.1.call-done, bf16[4096,768]{1,0:T(8,128)(2,1)} %all-gather.9.cloned.1.call-done), kind=kOutput, calls=%fused_computation.11 | convolution fusion | flops 2147483648 | bytes 11534336 | tf_op jit(solution)/shard_map/dot_general | solution.py:256
  211.3 1.2 fusion.15
  212.6 1.0 copy.46
  213.6 0.0 all-gather.15.cloned.1.call-update
  213.6 0.0 all-gather.11.cloned.1.call-start
  213.7 3.1 multiply_cosine_fusion
  216.8 41.8 %all-gather.15.cloned.1.call-done = bf16[4160,256]{1,0:T(8,128)(2,1)} async-done(((bf16[1040,256]{1,0:T(8,128)(2,1)}), bf16[4160,256]{1,0:T(8,128)(2,1)}) %all-gather.15.cloned.1.call-update) | async-done | bytes 2129936 | tf_op jit(solution)/shard_map/all_gather | solution.py:261
  258.6 1.7 slice.98
  260.3 0.0 all-gather.11.cloned.1.call-update
  260.3 0.2 all-gather.13.cloned.1.call-start
  260.6 8.3 %fusion = f32[1024,512]{0,1:T(8,128)S(1)} fusion(bf16[1024,4096]{1,0:T(8,128)(2,1)} %all-gather.7.cloned.1.call-done, bf16[4096,768]{1,0:T(8,128)(2,1)} %all-gather.9.cloned.1.call-done), kind=kOutput, calls=%fused_computation.1 | convolution fusion | flops 4294967296 | bytes 14680064 | tf_op jit(solution)/shard_map/dot_general | solution.py:267
  268.8 1.2 fusion.21
  270.0 2.7 copy.51
  272.7 1.8 copy.52
  274.5 3.0 subtract_convert_fusion
  277.5 1.4 pad_maximum_fusion.1
  278.9 0.2 copy.61
  279.1 0.8 slice_bitcast_fusion.1
  279.9 1.8 convert_reduce_fusion
  281.7 1.0 copy.49.start_ref
  282.8 0.2 fusion.18
  283.0 0.0 copy-start.1
  283.0 1.0 copy-done.1
  284.0 13.1 %shard_map.73 = bf16[1024,512]{1,0:T(8,128)(2,1)S(1)} custom-call(s32[4]{0:T(128)S(1)} %get-tuple-element.37.lo_ref, s32[4]{0:T(128)S(1)} %get-tuple-element.35.mid_ref, s32[4]{0:T(128)S(1)} %get-tuple-element.36.diag_ref, s32[4]{0:T(128)S(1)} %and_select_fusion.end_ref, s32[1]{0:T(128)} %bitcast.9.first_ref, bf16[1024,512]{1,0:T(8,128)(2,1)S(1)} %bitcast.44, ...), custom_call_target="tpu_custom_call" | custom-call | flops 34359738368 | bytes 134217728 | tf_op jit(solution)/shard_map/pallas_call | solution.py:217
  297.2 0.0 copy-start
  297.2 1.0 copy-done
  298.1 41.6 %all-gather.11.cloned.1.call-done = bf16[4096,512]{1,0:T(8,128)(2,1)} async-done(((bf16[4096,128]{1,0:T(8,128)(2,1)}), bf16[4096,512]{1,0:T(8,128)(2,1)}) %all-gather.11.cloned.1.call-update) | async-done | bytes 4194320 | tf_op jit(solution)/shard_map/all_gather | solution.py:272
  339.8 0.0 all-gather.13.cloned.1.call-update
  339.8 55.9 %all-gather.13.cloned.1.call-done = bf16[1024,4096]{1,0:T(8,128)(2,1)} async-done(((bf16[1024,512]{1,0:T(8,128)(2,1)}), bf16[1024,4096]{1,0:T(8,128)(2,1)}) %all-gather.13.cloned.1.call-update) | async-done | bytes 8388624 | tf_op jit(solution)/shard_map/all_gather | solution.py:275
  395.7 9.0 %convolution_convert_fusion = bf16[1024,512]{1,0:T(8,128)(2,1)S(1)} fusion(bf16[1024,4096]{1,0:T(8,128)(2,1)} %all-gather.13.cloned.1.call-done, bf16[4096,512]{1,0:T(8,128)(2,1)} %all-gather.11.cloned.1.call-done), kind=kOutput, calls=%fused_computation.16 | convolution fusion | flops 4295491584 | bytes 13631488 | tf_op jit(solution)/shard_map/dot_general | solution.py:276
  404.7 17.9 %all_to_all.27 = bf16[8,128,512]{2,1,0:T(8,128)(2,1)S(1)} all-to-all(bf16[8,128,512]{2,1,0:T(8,128)(2,1)S(1)} %bitcast.56), channel_id=1, replica_groups=mesh['grp'=1,'seq'=16,'head'=1,'srv'=2] {'seq':(4)4,'srv'}, dimensions={0} | all-to-all | bytes 2097152 | tf_op jit(solution)/shard_map/all_to_all | solution.py:277
  422.6 0.3 convert_bitcast_fusion
  422.9 1.8 reshape.216
  424.7 2.9 copy.50
  427.6 0.0 copy-done.3
  427.6 2.2 fusion.5
  (17 shorter events, 0.3 us)
Async XLA Ops:
  6.5 3.2 copy-start.4
  6.5 3.4 copy-start.5
  6.5 4.2 copy-start.2
  6.5 81.4 %all-gather.7.cloned.1.call-start = ((), (), s32[]{:S(2)}) async-start(), calls=%async_computation.2 | async-start | bytes 9437184 | tf_op jit(solution)/shard_map/all_gather | solution.py:245
  7.5 3.6 copy-start.6
  14.4 190.5 %all-gather.9.cloned.1.call-start = ((), (), s32[]{:S(2)}) async-start(), calls=%async_computation.3 | async-start | bytes 7864320 | tf_op jit(solution)/shard_map/all_gather | solution.py:251
  88.0 170.6 %all-gather.15.cloned.1.call-start = ((), (), s32[]{:S(2)}) async-start(), calls=%async_computation.6 | async-start | bytes 2662400 | tf_op jit(solution)/shard_map/all_gather | solution.py:261
  213.6 126.2 %all-gather.11.cloned.1.call-start = ((), (), s32[]{:S(2)}) async-start(), calls=%async_computation.4 | async-start | bytes 5242880 | tf_op jit(solution)/shard_map/all_gather | solution.py:272
  260.3 135.4 %all-gather.13.cloned.1.call-start = ((), (), s32[]{:S(2)}) async-start(), calls=%async_computation.5 | async-start | bytes 9437184 | tf_op jit(solution)/shard_map/all_gather | solution.py:275
  283.0 1.0 copy-start.1
  297.2 1.0 copy-start
  424.7 2.9 copy-start.3
Sparse Core Ops, SparseCore 0:
  14.5 73.3 all-gather.6
  89.5 115.3 all-gather.8
  213.7 44.7 all-gather.14
  260.4 79.2 all-gather.10
  341.5 54.1 all-gather.12

commit v3 on v2

--- a/solution.py
+++ b/solution.py
@@ -225,6 +225,24 @@
     )(low, mid, diag, end, jnp.reshape(first, (1,)), queries, keys_values, starts[:, None])
 
 
+def permuted(block, axis, partner):
+    count = lax.axis_size(axis)
+    return [
+        lax.ppermute(block, axis, [(i, partner(i, k)) for i in range(count)])
+        for k in range(1, count)
+    ]
+
+
+def laid(blocks, origins, dim):
+    size = blocks[0].shape[dim]
+    shape = list(blocks[0].shape)
+    shape[dim] = size * len(blocks)
+    whole = jnp.zeros(shape, blocks[0].dtype)
+    for block, origin in zip(blocks, origins):
+        whole = lax.dynamic_update_slice_in_dim(whole, block, origin * size, dim)
+    return whole
+
+
 def plane_local(tokens, norm_gain, wq, wk, wv, wo, doc_ids):
     tok_rows, model_width = tokens.shape
     plane = lax.axis_size("h")
@@ -242,12 +260,13 @@
     doc_rows = doc_rows.at[0, :, :tok_rows].set(doc_ids.astype(jnp.bfloat16))
     sent = jnp.concatenate([weights, doc_rows], axis=0)
     sent, normed = lax.optimization_barrier((sent, normed))
-    normed_all = lax.all_gather(normed, "h", axis=0, tiled=True)
+    me = lax.axis_index("h")
+    normed_blocks = [normed] + permuted(normed, "h", lambda i, k: i ^ k)
+    normed_all = laid(normed_blocks, [me ^ k for k in range(plane)], 0)
     landed = lax.all_to_all(sent.reshape(tok_rows + pack, -1), "h", 1, 0, tiled=True)
     landed = landed.reshape(plane, tok_rows + pack, -1)
     doc_plane = landed[:, tok_rows, :tok_rows].reshape(-1)
     w_mine = landed[:, :tok_rows].reshape(plane * tok_rows, -1)
-    w_mine, normed_all = lax.optimization_barrier((w_mine, normed_all))
     w_all = lax.all_gather(w_mine, "z", axis=0, tiled=True)
 
     plane_rows = tok_rows * plane
@@ -268,10 +287,12 @@
     queries = rope(query_acc.reshape(plane_rows, -1, HEAD_WIDTH), positions)
     queries = queries.astype(jnp.bfloat16).reshape(plane_rows, -1)
 
-    wo, kv_all = lax.optimization_barrier((wo, kv_all))
-    wo_all = lax.all_gather(wo, "z", axis=1, tiled=True)
+    wo, kv_all, starts, queries = lax.optimization_barrier((wo, kv_all, starts, queries))
+    moved = permuted(wo, "z", lambda i, k: (i + k) % planes)
     attended = attend(queries, kv_all, starts, first_pos, 256, 512)
-    attended, wo_all = lax.optimization_barrier((attended, wo_all))
+    attended, moved[0], moved[-1] = lax.optimization_barrier((attended, moved[0], moved[-1]))
+    level = lax.axis_index("z")
+    wo_all = laid([wo] + moved, [(level - k) % planes for k in range(planes)], 1)
     attended_all = lax.all_gather(attended, "h", axis=1, tiled=True)
     terms = jnp.dot(attended_all, wo_all, preferred_element_type=jnp.float32).astype(jnp.bfloat16)
     rows_mine = lax.all_to_all(terms, "h", 0, 1, tiled=True)

time: 437 us -> 367 us (0.84)
  waiting for transfers between devices: 286 us -> 188 us
  local copies, waits for them, and re-layouts: 24.8 us -> 53.7 us
  blocking collectives: 57.4 us -> 46.3 us
  starting transfers between devices: 0.35 us -> 10 us
    ppermute x0 -> x10, waiting for transfers between devices: none -> 143 us  [permuted(): lax.ppermute(block, axis, [(i, partner(i, k)) for i in range(count)])]
    all_gather x1, waiting for transfers between devices: 117 us -> 15.8 us  [plane_local(): w_all = lax.all_gather(w_mine, 'z', axis=0, tiled=True)]
    all_gather x2 -> x0, waiting for transfers between devices: 71.9 us -> none  [the longest x1 41.6 us: plane_local(): wo_all = lax.all_gather(wo, 'z', axis=1, tiled=True)]
    all_gather x1, waiting for transfers between devices: 55.9 us -> 4.65 us  [plane_local(): attended_all = lax.all_gather(attended, 'h', axis=1, tiled=True)]
    dynamic_update_slice x0 -> x12, local copies, waits for them, and re-layouts: none -> 21.9 us  [laid(): whole = lax.dynamic_update_slice_in_dim(whole, block, origin * size, dim)]
    all_gather x1, waiting for transfers between devices: 41.8 us -> 24 us  [plane_local(): lax.all_gather(jnp.concatenate([kv_mine, doc_fold], axis=0), 'z', axis=0)]
    all_to_all x1, blocking collectives: 39.5 us -> 28.4 us  [plane_local(): lax.all_to_all(sent.reshape(tok_rows + pack, -1), 'h', 1, 0, tiled=True)]
    ppermute x0 -> x10, starting transfers between devices: none -> 9.76 us  [permuted(): lax.ppermute(block, axis, [(i, partner(i, k)) for i in range(count)])]
  transfers between devices with their start and end apart: 5 -> 13, of which waited for: 5 -> 9; matrix products, arithmetic and copies ran while one was open for 7% -> 14% of each run, Pallas kernels for 3% -> 4%
where the time goes in v3:
time: 367 us; the launch traced here: 366 us
  waiting for transfers between devices  188 us (51%)
  local copies, waits for them, and re-layouts  53.7 us (15%)
  blocking collectives  46.3 us (13%)
  matrix products  24 us (7%)
  other arithmetic  17.1 us (5%)
  Pallas kernels  13.6 us (4%)
  between operations  13.4 us (4%)
  starting transfers between devices  10 us (3%)
    ppermute x10, waiting for transfers between devices, permuted(): lax.ppermute(block, axis, [(i, partner(i, k)) for i in range(count)])  143 us
    all_to_all x1, blocking collectives, plane_local(): lax.all_to_all(sent.reshape(tok_rows + pack, -1), 'h', 1, 0, tiled=True)  28.4 us
    all_gather x1, waiting for transfers between devices, plane_local(): lax.all_gather(jnp.concatenate([kv_mine, doc_fold], axis=0), 'z', axis=0)  24 us
    dynamic_update_slice x12, local copies, waits for them, and re-layouts, laid(): whole = lax.dynamic_update_slice_in_dim(whole, block, origin * size, dim)  21.9 us
    all_to_all x1, blocking collectives, plane_local(): rows_mine = lax.all_to_all(terms, 'h', 0, 1, tiled=True)  17.9 us
    all_gather x1, waiting for transfers between devices, plane_local(): w_all = lax.all_gather(w_mine, 'z', axis=0, tiled=True)  15.8 us
    pallas_call x1, Pallas kernels, attend(): pl.pallas_call(functools.partial(attention_kernel, head_count, key_block)...  13.6 us
    unnamed x27, local copies, waits for them, and re-layouts  11 us
  transfers between devices with their start and end apart: 13, of which 9 were waited for; matrix products, arithmetic and copies ran while one was open for 14% of the time, Pallas kernels for 4%

profile of v3, /device:TPU:0, one launch (start us, length us, event | category | flops | bytes accessed | tf_op | source)
XLA Modules:
  0.0 366.0 jit_solution(11706801431999438587)
XLA Ops:
  6.5 0.7 convert_bitcast_fusion.1
  7.4 1.1 copy.42
  8.6 1.8 copy.41
  10.4 2.3 copy.40
  12.6 1.6 fusion.2
  14.3 1.3 fusion.4
  15.6 0.2 scatter.8
  15.8 0.7 pad_maximum_fusion
  16.5 2.5 copy.44
  19.0 28.4 %all_to_all.26 = bf16[144,8,768]{2,0,1:T(8,128)(2,1)S(1)} all-to-all(bf16[144,8,768]{2,0,1:T(8,128)(2,1)} %copy.44), channel_id=1, replica_groups=mesh['grp'=1,'seq'=16,'head'=1,'srv'=2] {'seq':(4)4,'srv'}, dimensions={1} | all-to-all | bytes 3538944 | tf_op jit(solution)/shard_map/all_to_all | solution.py:266
  47.4 1.3 slice.84
  48.8 0.6 collective-permute-start.1
  49.4 1.2 collective-permute-start.2
  50.7 0.6 collective-permute-start.3
  51.2 1.1 collective-permute-start.4
  52.4 4.9 %broadcast_in_dim.8 = bf16[1024,4096]{1,0:T(8,128)(2,1)} broadcast(bf16[]{:T(256)} %constant.121.clone.1), dimensions={} | broadcast | bytes 8388610 | tf_op jit(solution)/shard_map/broadcast_in_dim | solution.py:240
  57.2 1.0 constant_dynamic-update-slice_fusion.11
  58.4 2.4 constant_dynamic-update-slice_fusion.10
  60.8 14.2 %collective-permute-done.1 = bf16[128,4096]{1,0:T(8,128)(2,1)} collective-permute-done((bf16[128,4096]{1,0:T(8,128)(2,1)S(1)}, bf16[128,4096]{1,0:T(8,128)(2,1)}, u32[]{:S(2)}, u32[]{:S(2)}) %collective-permute-start.1) | collective-permute-done | bytes 1048608 | tf_op jit(solution)/shard_map/ppermute | solution.py:231
  74.9 2.3 constant_dynamic-update-slice_fusion.9
  77.2 19.3 %collective-permute-done.2 = bf16[128,4096]{1,0:T(8,128)(2,1)} collective-permute-done((bf16[128,4096]{1,0:T(8,128)(2,1)S(1)}, bf16[128,4096]{1,0:T(8,128)(2,1)}, u32[]{:S(2)}, u32[]{:S(2)}) %collective-permute-start.2) | collective-permute-done | bytes 1048608 | tf_op jit(solution)/shard_map/ppermute | solution.py:231
  96.5 2.3 constant_dynamic-update-slice_fusion.8
  98.8 2.3 constant_dynamic-update-slice_fusion.7
  101.1 41.9 %collective-permute-done.4 = bf16[128,4096]{1,0:T(8,128)(2,1)} collective-permute-done((bf16[128,4096]{1,0:T(8,128)(2,1)S(1)}, bf16[128,4096]{1,0:T(8,128)(2,1)}, u32[]{:S(2)}, u32[]{:S(2)}) %collective-permute-start.4) | collective-permute-done | bytes 1048608 | tf_op jit(solution)/shard_map/ppermute | solution.py:231
  143.0 2.3 constant_dynamic-update-slice_fusion.6
  145.4 1.1 constant_dynamic-update-slice_fusion.5
  146.4 1.1 constant_dynamic-update-slice_fusion.4
  147.7 15.8 %all-gather.5.cloned.1.call-done = bf16[4096,768]{1,0:T(8,128)(2,1)} async-done(((bf16[1024,768]{1,0:T(8,128)(2,1)}), bf16[4096,768]{1,0:T(8,128)(2,1)}) %all-gather.5.cloned.1.call-update) | async-done | bytes 6291472 | tf_op jit(solution)/shard_map/all_gather | solution.py:270
  163.6 6.3 %fusion.6 = f32[1024,256]{0,1:T(8,128)S(1)} fusion(bf16[1024,4096]{1,0:T(8,128)(2,1)} %constant_dynamic-update-slice_fusion.4, bf16[4096,768]{1,0:T(8,128)(2,1)} %all-gather.5.cloned.1.call-done), kind=kOutput, calls=%fused_computation.11 | convolution fusion | flops 2147483648 | bytes 11534336 | tf_op jit(solution)/shard_map/dot_general | solution.py:275
  170.0 1.2 fusion.15
  171.2 1.0 copy.46
  172.3 0.2 all-gather.7.cloned.1.call-start
  172.5 3.1 multiply_cosine_fusion
  175.6 8.6 %fusion = f32[1024,512]{0,1:T(8,128)S(1)} fusion(bf16[1024,4096]{1,0:T(8,128)(2,1)} %constant_dynamic-update-slice_fusion.4, bf16[4096,768]{1,0:T(8,128)(2,1)} %all-gather.5.cloned.1.call-done), kind=kOutput, calls=%fused_computation.1 | convolution fusion | flops 4294967296 | bytes 14680064 | tf_op jit(solution)/shard_map/dot_general | solution.py:286
  184.2 1.2 fusion.21
  185.4 1.9 copy.52
  187.3 1.8 copy.51
  189.0 2.6 subtract_convert_fusion
  191.6 1.4 pad_maximum_fusion.1
  193.2 24.0 %all-gather.9.cloned.1.call-done = bf16[4160,256]{1,0:T(8,128)(2,1)} async-done(((bf16[1040,256]{1,0:T(8,128)(2,1)}), bf16[4160,256]{1,0:T(8,128)(2,1)}) %all-gather.9.cloned.1.call-update) | async-done | bytes 2129936 | tf_op jit(solution)/shard_map/all_gather | solution.py:280
  217.2 1.7 slice.91
  219.0 0.8 slice_bitcast_fusion.1
  219.8 1.8 convert_reduce_fusion
  221.6 3.8 %collective-permute-start.8 = (bf16[4096,128]{1,0:T(8,128)(2,1)}, bf16[4096,128]{1,0:T(8,128)(2,1)}, u32[]{:S(2)}, u32[]{:S(2)}) collective-permute-start(bf16[4096,128]{1,0:T(8,128)(2,1)} %param.14), channel_id=1, source_target_pairs={{0,24},{8,0},{16,8},{24,16},{1,25},{9,1},{17,9},{25,17},{2,26},{10... | collective-permute-start | bytes 3145736 | tf_op jit(solution)/shard_map/ppermute | solution.py:231
  225.5 0.2 fusion.18
  225.6 1.0 copy.49.start_ref
  226.7 1.0 copy-done
  227.7 13.6 %shard_map.73 = bf16[1024,512]{1,0:T(8,128)(2,1)} custom-call(s32[4]{0:T(128)S(1)} %get-tuple-element.39.lo_ref, s32[4]{0:T(128)S(1)} %get-tuple-element.37.mid_ref, s32[4]{0:T(128)S(1)} %get-tuple-element.38.diag_ref, s32[4]{0:T(128)S(1)} %and_select_fusion.end_ref, s32[1]{0:T(128)} %bitcast.11.first_ref, bf16[1024,512]{1,0:T(8,128)(2,1)S(1)} %bitcast.44, ...), custom_call_target="tpu_custom_call" | custom-call | flops 34359738368 | bytes 134217728 | tf_op jit(solution)/shard_map/pallas_call | solution.py:217
  241.4 8.4 %collective-permute-done.7 = bf16[4096,128]{1,0:T(8,128)(2,1)} collective-permute-done((bf16[4096,128]{1,0:T(8,128)(2,1)}, bf16[4096,128]{1,0:T(8,128)(2,1)}, u32[]{:S(2)}, u32[]{:S(2)}) %collective-permute-start.7) | collective-permute-done | bytes 1048608 | tf_op jit(solution)/shard_map/ppermute | solution.py:231
  249.8 19.8 %collective-permute-done.8 = bf16[4096,128]{1,0:T(8,128)(2,1)} collective-permute-done((bf16[4096,128]{1,0:T(8,128)(2,1)}, bf16[4096,128]{1,0:T(8,128)(2,1)}, u32[]{:S(2)}, u32[]{:S(2)}) %collective-permute-start.8) | collective-permute-done | bytes 1048608 | tf_op jit(solution)/shard_map/ppermute | solution.py:231
  269.6 2.2 collective-permute-start.9
  271.8 2.2 broadcast_in_dim.11
  274.0 1.1 constant_dynamic-update-slice_fusion.3
  275.1 2.4 constant_dynamic-update-slice_fusion.2
  277.5 39.7 %collective-permute-done.9 = bf16[4096,128]{1,0:T(8,128)(2,1)S(1)} collective-permute-done((bf16[4096,128]{1,0:T(8,128)(2,1)}, bf16[4096,128]{1,0:T(8,128)(2,1)S(1)}, u32[]{:S(2)}, u32[]{:S(2)}) %collective-permute-start.9) | collective-permute-done | bytes 1048608 | tf_op jit(solution)/shard_map/ppermute | solution.py:231
  317.3 1.1 constant_dynamic-update-slice_fusion.1
  318.4 2.4 constant_dynamic-update-slice_fusion
  320.8 4.7 %all-gather.7.cloned.1.call-done = bf16[1024,4096]{1,0:T(8,128)(2,1)} async-done(((bf16[1024,512]{1,0:T(8,128)(2,1)}), bf16[1024,4096]{1,0:T(8,128)(2,1)}) %all-gather.7.cloned.1.call-update) | async-done | bytes 8388624 | tf_op jit(solution)/shard_map/all_gather | solution.py:296
  325.5 9.1 %convolution_convert_fusion = bf16[1024,512]{1,0:T(8,128)(2,1)S(1)} fusion(bf16[1024,4096]{1,0:T(8,128)(2,1)} %all-gather.7.cloned.1.call-done, bf16[4096,512]{1,0:T(8,128)(2,1)} %constant_dynamic-update-slice_fusion), kind=kOutput, calls=%fused_computation.16 | convolution fusion | flops 4295491584 | bytes 13631488 | tf_op jit(solution)/shard_map/dot_general | solution.py:297
  334.5 17.9 %all_to_all.27 = bf16[8,128,512]{2,1,0:T(8,128)(2,1)S(1)} all-to-all(bf16[8,128,512]{2,1,0:T(8,128)(2,1)S(1)} %bitcast.56), channel_id=1, replica_groups=mesh['grp'=1,'seq'=16,'head'=1,'srv'=2] {'seq':(4)4,'srv'}, dimensions={0} | all-to-all | bytes 2097152 | tf_op jit(solution)/shard_map/all_to_all | solution.py:298
  352.4 0.3 convert_bitcast_fusion
  352.7 1.8 reshape.216
  354.5 2.8 copy.50
  357.3 2.2 fusion.5
  (47 shorter events, 1.1 us)
Async XLA Ops:
  6.5 7.8 %copy-start.1 = (bf16[128,4096]{1,0:T(8,128)(2,1)S(1)}, bf16[128,4096]{1,0:T(8,128)(2,1)}, u32[]{:S(2)}) copy-start(bf16[128,4096]{1,0:T(8,128)(2,1)} %param.9) | copy-start | bytes 3145732
  6.5 7.8 %copy-start.7 = (f32[4096]{0:T(1024)S(1)}, f32[4096]{0:T(1024)}, u32[]{:S(2)}) copy-start(f32[4096]{0:T(1024)} %param.10) | copy-start | bytes 49156
  6.5 157.0 %all-gather.5.cloned.1.call-start = ((), (), s32[]{:S(2)}) async-start(), calls=%async_computation.2 | async-start | bytes 7864320 | tf_op jit(solution)/shard_map/all_gather | solution.py:270
  12.6 3.2 copy-start.4
  12.6 3.2 copy-start.6
  19.0 29.7 %copy-start.3 = (bf16[128,4096]{1,0:T(8,128)(2,1)S(1)}, bf16[128,4096]{1,0:T(8,128)(2,1)}, u32[]{:S(2)}) copy-start(bf16[128,4096]{1,0:T(8,128)(2,1)} %fusion.4) | copy-start | bytes 3145732
  48.7 168.6 %all-gather.9.cloned.1.call-start = ((), (), s32[]{:S(2)}) async-start(), calls=%async_computation.4 | async-start | bytes 2662400 | tf_op jit(solution)/shard_map/all_gather | solution.py:280
  48.7 9.6 %collective-permute-start = (bf16[128,4096]{1,0:T(8,128)(2,1)S(1)}, bf16[128,4096]{1,0:T(8,128)(2,1)}, u32[]{:S(2)}, u32[]{:S(2)}) collective-permute-start(bf16[128,4096]{1,0:T(8,128)(2,1)S(1)} %copy-done.3), channel_id=1, source_target_pairs={{0,1},{1,0},{2,3},{3,2},{4,5},{5,4},{6,7},{7,6},{8,9},{9,8},{10,11... | collective-permute-start | bytes 3145736 | tf_op jit(solution)/shard_map/ppermute | solution.py:231
  48.8 26.1 %collective-permute-start.1 = (bf16[128,4096]{1,0:T(8,128)(2,1)S(1)}, bf16[128,4096]{1,0:T(8,128)(2,1)}, u32[]{:S(2)}, u32[]{:S(2)}) collective-permute-start(bf16[128,4096]{1,0:T(8,128)(2,1)S(1)} %copy-done.3), channel_id=1, source_target_pairs={{0,2},{1,3},{2,0},{3,1},{4,6},{5,7},{6,4},{7,5},{8,10},{9,11},{10,... | collective-permute-start | bytes 3145736 | tf_op jit(solution)/shard_map/ppermute | solution.py:231
  49.4 47.1 %collective-permute-start.2 = (bf16[128,4096]{1,0:T(8,128)(2,1)S(1)}, bf16[128,4096]{1,0:T(8,128)(2,1)}, u32[]{:S(2)}, u32[]{:S(2)}) collective-permute-start(bf16[128,4096]{1,0:T(8,128)(2,1)S(1)} %copy-done.3), channel_id=1, source_target_pairs={{0,3},{1,2},{2,1},{3,0},{4,7},{5,6},{6,5},{7,4},{8,11},{9,10},{10,... | collective-permute-start | bytes 3145736 | tf_op jit(solution)/shard_map/ppermute | solution.py:231
  50.7 48.2 %collective-permute-start.3 = (bf16[128,4096]{1,0:T(8,128)(2,1)S(1)}, bf16[128,4096]{1,0:T(8,128)(2,1)}, u32[]{:S(2)}, u32[]{:S(2)}) collective-permute-start(bf16[128,4096]{1,0:T(8,128)(2,1)S(1)} %copy-done.3), channel_id=1, source_target_pairs={{0,4},{1,5},{2,6},{3,7},{4,0},{5,1},{6,2},{7,3},{8,12},{9,13},{10,... | collective-permute-start | bytes 3145736 | tf_op jit(solution)/shard_map/ppermute | solution.py:231
  51.2 91.8 %collective-permute-start.4 = (bf16[128,4096]{1,0:T(8,128)(2,1)S(1)}, bf16[128,4096]{1,0:T(8,128)(2,1)}, u32[]{:S(2)}, u32[]{:S(2)}) collective-permute-start(bf16[128,4096]{1,0:T(8,128)(2,1)S(1)} %copy-done.3), channel_id=1, source_target_pairs={{0,5},{1,4},{2,7},{3,6},{4,1},{5,0},{6,3},{7,2},{8,13},{9,12},{10,... | collective-permute-start | bytes 3145736 | tf_op jit(solution)/shard_map/ppermute | solution.py:231
  58.3 87.1 %collective-permute-start.5 = (bf16[128,4096]{1,0:T(8,128)(2,1)S(1)}, bf16[128,4096]{1,0:T(8,128)(2,1)S(1)}, u32[]{:S(2)}, u32[]{:S(2)}) collective-permute-start(bf16[128,4096]{1,0:T(8,128)(2,1)S(1)} %copy-done.3), channel_id=1, source_target_pairs={{0,6},{1,7},{2,4},{3,5},{4,2},{5,3},{6,0},{7,1},{8,14},{9,15},{10,... | collective-permute-start | bytes 3145736 | tf_op jit(solution)/shard_map/ppermute | solution.py:231
  74.9 71.5 %collective-permute-start.6 = (bf16[128,4096]{1,0:T(8,128)(2,1)S(1)}, bf16[128,4096]{1,0:T(8,128)(2,1)S(1)}, u32[]{:S(2)}, u32[]{:S(2)}) collective-permute-start(bf16[128,4096]{1,0:T(8,128)(2,1)S(1)} %copy-done.3), channel_id=1, source_target_pairs={{0,7},{1,6},{2,5},{3,4},{4,3},{5,2},{6,1},{7,0},{8,15},{9,14},{10,... | collective-permute-start | bytes 3145736 | tf_op jit(solution)/shard_map/ppermute | solution.py:231
  172.3 153.2 %all-gather.7.cloned.1.call-start = ((), (), s32[]{:S(2)}) async-start(), calls=%async_computation.3 | async-start | bytes 9437184 | tf_op jit(solution)/shard_map/all_gather | solution.py:296
  221.6 28.2 %collective-permute-start.7 = (bf16[4096,128]{1,0:T(8,128)(2,1)}, bf16[4096,128]{1,0:T(8,128)(2,1)}, u32[]{:S(2)}, u32[]{:S(2)}) collective-permute-start(bf16[4096,128]{1,0:T(8,128)(2,1)} %param.14), channel_id=1, source_target_pairs={{0,8},{8,16},{16,24},{24,0},{1,9},{9,17},{17,25},{25,1},{2,10},{10... | collective-permute-start | bytes 3145736 | tf_op jit(solution)/shard_map/ppermute | solution.py:231
  221.6 48.0 %collective-permute-start.8 = (bf16[4096,128]{1,0:T(8,128)(2,1)}, bf16[4096,128]{1,0:T(8,128)(2,1)}, u32[]{:S(2)}, u32[]{:S(2)}) collective-permute-start(bf16[4096,128]{1,0:T(8,128)(2,1)} %param.14), channel_id=1, source_target_pairs={{0,24},{8,0},{16,8},{24,16},{1,25},{9,1},{17,9},{25,17},{2,26},{10... | collective-permute-start | bytes 3145736 | tf_op jit(solution)/shard_map/ppermute | solution.py:231
  226.7 1.0 copy-start
  241.4 32.7 %copy-start.5 = (bf16[4096,128]{1,0:T(8,128)(2,1)S(1)}, bf16[4096,128]{1,0:T(8,128)(2,1)}, u32[]{:S(2)}) copy-start(bf16[4096,128]{1,0:T(8,128)(2,1)} %param.14) | copy-start | bytes 3145732
  269.6 47.7 %collective-permute-start.9 = (bf16[4096,128]{1,0:T(8,128)(2,1)}, bf16[4096,128]{1,0:T(8,128)(2,1)S(1)}, u32[]{:S(2)}, u32[]{:S(2)}) collective-permute-start(bf16[4096,128]{1,0:T(8,128)(2,1)} %param.14), channel_id=1, source_target_pairs={{0,16},{8,24},{16,0},{24,8},{1,17},{9,25},{17,1},{25,9},{2,18},{10... | collective-permute-start | bytes 3145736 | tf_op jit(solution)/shard_map/ppermute | solution.py:231
  352.7 4.6 %copy-start.2 = (bf16[128,4096]{1,0:T(8,128)(2,1)S(1)}, bf16[128,4096]{1,0:T(8,128)(2,1)}, u32[]{:S(2)}) copy-start(bf16[128,4096]{1,0:T(8,128)(2,1)} %param.9) | copy-start | bytes 3145732
Sparse Core Ops, SparseCore 0:
  48.8 114.7 all-gather.4
  172.4 44.7 all-gather.8
  269.7 55.6 all-gather.6

commit v4 on v3

--- a/solution.py
+++ b/solution.py
@@ -220,16 +220,16 @@
         grid_spec=spec,
         compiler_params=pltpu.CompilerParams(vmem_limit_bytes=48 * 1024 * 1024),
         cost_estimate=pl.CostEstimate(
-            flops=32 * pairs * HEAD_WIDTH, bytes_accessed=128 << 20, transcendentals=pairs
+            flops=32 * pairs * HEAD_WIDTH, bytes_accessed=64 << 20, transcendentals=pairs
         ),
     )(low, mid, diag, end, jnp.reshape(first, (1,)), queries, keys_values, starts[:, None])
 
 
-def permuted(block, axis, partner):
+def permuted(block, axis, partner, steps):
     count = lax.axis_size(axis)
     return [
         lax.ppermute(block, axis, [(i, partner(i, k)) for i in range(count)])
-        for k in range(1, count)
+        for k in steps
     ]
 
 
@@ -261,9 +261,12 @@
     sent = jnp.concatenate([weights, doc_rows], axis=0)
     sent, normed = lax.optimization_barrier((sent, normed))
     me = lax.axis_index("h")
-    normed_blocks = [normed] + permuted(normed, "h", lambda i, k: i ^ k)
+    normed_blocks = [normed] + permuted(normed, "h", lambda i, k: i ^ k, range(1, plane))
     normed_all = laid(normed_blocks, [me ^ k for k in range(plane)], 0)
     landed = lax.all_to_all(sent.reshape(tok_rows + pack, -1), "h", 1, 0, tiled=True)
+    ahead = lambda i, k: (i + k) % planes
+    outer = permuted(wo, "z", ahead, (1, planes - 1))
+    landed, outer = lax.optimization_barrier((landed, outer))
     landed = landed.reshape(plane, tok_rows + pack, -1)
     doc_plane = landed[:, tok_rows, :tok_rows].reshape(-1)
     w_mine = landed[:, :tok_rows].reshape(plane * tok_rows, -1)
@@ -272,6 +275,8 @@
     plane_rows = tok_rows * plane
     positions = first_pos + jnp.arange(plane_rows, dtype=jnp.int32)
 
+    wo_late, w_all = lax.optimization_barrier((wo, w_all))
+    inner = permuted(wo_late, "z", ahead, range(2, planes - 1))
     kv_acc = jnp.dot(normed_all, w_all[:, width:], preferred_element_type=jnp.float32)
     keys = rope(kv_acc[:, None, :HEAD_WIDTH], positions)[:, 0]
     kv_mine = jnp.concatenate([keys, kv_acc[:, HEAD_WIDTH:]], axis=1).astype(jnp.bfloat16)
@@ -287,14 +292,20 @@
     queries = rope(query_acc.reshape(plane_rows, -1, HEAD_WIDTH), positions)
     queries = queries.astype(jnp.bfloat16).reshape(plane_rows, -1)
 
-    wo, kv_all, starts, queries = lax.optimization_barrier((wo, kv_all, starts, queries))
-    moved = permuted(wo, "z", lambda i, k: (i + k) % planes)
-    attended = attend(queries, kv_all, starts, first_pos, 256, 512)
-    attended, moved[0], moved[-1] = lax.optimization_barrier((attended, moved[0], moved[-1]))
+    inner, kv_all, starts, queries = lax.optimization_barrier((inner, kv_all, starts, queries))
+    moved = [outer[0]] + inner + [outer[1]]
+    half = plane_rows // 2
+    block_rows = math.gcd(half, 256)
+    lower = attend(queries[:half], kv_all, starts[:half], first_pos, block_rows, 512)
+    lower, upper_queries = lax.optimization_barrier((lower, queries[half:]))
+    lower_all = lax.all_gather(lower, "h", axis=1, tiled=True)
+    upper = attend(upper_queries, kv_all, starts[half:], first_pos + half, block_rows, 512)
+    upper_all = lax.all_gather(upper, "h", axis=1, tiled=True)
     level = lax.axis_index("z")
     wo_all = laid([wo] + moved, [(level - k) % planes for k in range(planes)], 1)
-    attended_all = lax.all_gather(attended, "h", axis=1, tiled=True)
-    terms = jnp.dot(attended_all, wo_all, preferred_element_type=jnp.float32).astype(jnp.bfloat16)
+    lower_terms = jnp.dot(lower_all, wo_all, preferred_element_type=jnp.float32)
+    upper_terms = jnp.dot(upper_all, wo_all, preferred_element_type=jnp.float32)
+    terms = jnp.concatenate([lower_terms, upper_terms], axis=0).astype(jnp.bfloat16)
     rows_mine = lax.all_to_all(terms, "h", 0, 1, tiled=True)
     summed = rows_mine.reshape(tok_rows, plane, planes, -1).transpose(0, 2, 1, 3)
     summed = summed.reshape(tok_rows, model_width).astype(jnp.float32)
@@ -314,7 +325,7 @@
 
 
 def solution(mesh):
-    if mesh.shape["grp"] == 1 and mesh.shape["head"] == 1 and mesh.size % KV_HEAD_COUNT == 0:
+    if mesh.shape["grp"] == 1 and mesh.shape["head"] == 1 and mesh.size == 4 * KV_HEAD_COUNT:
         return plane_solution(mesh, mesh.size // KV_HEAD_COUNT)
     in_specs = (
         P(("grp", "seq", "srv"), "head"),

time: 367 us -> 431 us (1.17)
  waiting for transfers between devices: 188 us -> 269 us
  blocking collectives: 46.3 us -> 17.9 us
  starting transfers between devices: 10 us -> 17.4 us
    all_gather x1 -> x2, waiting for transfers between devices: 4.65 us -> 72.4 us  [the longest x1 39 us: plane_local(): lower_all = lax.all_gather(lower, 'h', axis=1, tiled=True)]
    all_gather x1, waiting for transfers between devices: 24 us -> 57.5 us  [plane_local(): lax.all_gather(jnp.concatenate([kv_mine, doc_fold], axis=0), 'z', axis=0)]
    all_to_all x1 -> x0, blocking collectives: 28.4 us -> none  [plane_local(): lax.all_to_all(sent.reshape(tok_rows + pack, -1), 'h', 1, 0, tiled=True)]
    ppermute x10, waiting for transfers between devices: 143 us -> 122 us  [permuted(): lax.ppermute(block, axis, [(i, partner(i, k)) for i in range(count)])]
    all_to_all x0 -> x1, starting transfers between devices: none -> 5.3 us  [plane_local(): lax.all_to_all(sent.reshape(tok_rows + pack, -1), 'h', 1, 0, tiled=True)]
    dot_general x1 -> x2, matrix products: 9.05 us -> 11.6 us  [the longest x1 5.79 us: plane_local(): lower_terms = jnp.dot(lower_all, wo_all, preferred_element_type=jnp.float32)]
    unnamed x27 -> x37, local copies, waits for them, and re-layouts: 11 us -> 12.9 us
    pallas_call x1 -> x2, Pallas kernels: 13.6 us -> 13.2 us  [attend(): pl.pallas_call(functools.partial(attention_kernel, head_count, key_block)...]
  transfers between devices with their start and end apart: 13 -> 15, of which waited for: 9 -> 10; matrix products, arithmetic and copies ran while one was open for 14% -> 14% of each run, Pallas kernels for 4% -> 2%
where the time goes in v4:
time: 431 us; the launch traced here: 428 us
  waiting for transfers between devices  269 us (62%)
  local copies, waits for them, and re-layouts  53.4 us (12%)
  matrix products  26.5 us (6%)
  blocking collectives  17.9 us (4%)
  starting transfers between devices  17.4 us (4%)
  other arithmetic  17.3 us (4%)
  between operations  13.5 us (3%)
  Pallas kernels  13.2 us (3%)
    ppermute x10, waiting for transfers between devices, permuted(): lax.ppermute(block, axis, [(i, partner(i, k)) for i in range(count)])  122 us
    all_gather x1, waiting for transfers between devices, plane_local(): lax.all_gather(jnp.concatenate([kv_mine, doc_fold], axis=0), 'z', axis=0)  57.5 us
    all_gather x1, waiting for transfers between devices, plane_local(): lower_all = lax.all_gather(lower, 'h', axis=1, tiled=True)  39 us
    all_gather x1, waiting for transfers between devices, plane_local(): upper_all = lax.all_gather(upper, 'h', axis=1, tiled=True)  33.4 us
    dynamic_update_slice x12, local copies, waits for them, and re-layouts, laid(): whole = lax.dynamic_update_slice_in_dim(whole, block, origin * size, dim)  20.5 us
    all_to_all x1, blocking collectives, plane_local(): rows_mine = lax.all_to_all(terms, 'h', 0, 1, tiled=True)  17.9 us
    all_gather x1, waiting for transfers between devices, plane_local(): w_all = lax.all_gather(w_mine, 'z', axis=0, tiled=True)  17.8 us
    pallas_call x2, Pallas kernels, attend(): pl.pallas_call(functools.partial(attention_kernel, head_count, key_block)...  13.2 us
  transfers between devices with their start and end apart: 15, of which 10 were waited for; matrix products, arithmetic and copies ran while one was open for 14% of the time, Pallas kernels for 2%

profile of v4, /device:TPU:0, one launch (start us, length us, event | category | flops | bytes accessed | tf_op | source)
XLA Modules:
  0.0 428.5 jit_solution(5642768186888425612)
XLA Ops:
  6.5 0.7 convert_bitcast_fusion.1
  7.4 2.3 copy.46
  9.7 1.1 copy.47
  10.8 1.8 copy.48
  12.6 1.6 fusion.2
  14.3 1.3 fusion.4
  15.8 0.7 pad_maximum_fusion
  16.5 2.5 copy.50
  19.0 5.3 %all-to-all-start = ((bf16[144,8,768]{2,0,1:T(8,128)(2,1)}), bf16[144,8,768]{2,0,1:T(8,128)(2,1)S(1)}, u32[]{:S(2)}, u32[]{:S(2)}) async-start(bf16[144,8,768]{2,0,1:T(8,128)(2,1)} %copy.50), calls=%async_computation | async-start | bytes 3538944 | tf_op jit(solution)/shard_map/all_to_all | solution.py:266
  24.3 1.6 collective-permute-start
  25.9 2.2 collective-permute-start.1
  28.2 24.2 %collective-permute-done = bf16[4096,128]{1,0:T(8,128)(2,1)S(1)} collective-permute-done((bf16[4096,128]{1,0:T(8,128)(2,1)}, bf16[4096,128]{1,0:T(8,128)(2,1)S(1)}, u32[]{:S(2)}, u32[]{:S(2)}) %collective-permute-start) | collective-permute-done | bytes 1048608 | tf_op jit(solution)/shard_map/ppermute | solution.py:231
  52.4 1.0 copy-done.6
  53.3 20.6 %collective-permute-done.1 = bf16[4096,128]{1,0:T(8,128)(2,1)} collective-permute-done((bf16[4096,128]{1,0:T(8,128)(2,1)}, bf16[4096,128]{1,0:T(8,128)(2,1)}, u32[]{:S(2)}, u32[]{:S(2)}) %collective-permute-start.1) | collective-permute-done | bytes 1048608 | tf_op jit(solution)/shard_map/ppermute | solution.py:231
  73.9 1.3 slice.130
  75.4 1.7 collective-permute-start.4
  77.3 1.6 collective-permute-start.6
  79.0 4.4 %broadcast_in_dim.10 = bf16[1024,4096]{1,0:T(8,128)(2,1)} broadcast(bf16[]{:T(256)} %constant.154.clone.1), dimensions={} | broadcast | bytes 8388610 | tf_op jit(solution)/shard_map/broadcast_in_dim | solution.py:240
  83.3 1.0 constant_dynamic-update-slice_fusion.11
  84.4 2.6 collective-permute-start.8
  87.0 2.4 constant_dynamic-update-slice_fusion.10
  89.4 12.1 %collective-permute-done.4 = bf16[128,4096]{1,0:T(8,128)(2,1)} collective-permute-done((bf16[128,4096]{1,0:T(8,128)(2,1)S(1)}, bf16[128,4096]{1,0:T(8,128)(2,1)}, u32[]{:S(2)}, u32[]{:S(2)}) %collective-permute-start.4) | collective-permute-done | bytes 1048608 | tf_op jit(solution)/shard_map/ppermute | solution.py:231
  101.5 1.4 collective-permute-start.9
  102.9 2.4 constant_dynamic-update-slice_fusion.9
  105.3 17.8 %collective-permute-done.5 = bf16[128,4096]{1,0:T(8,128)(2,1)} collective-permute-done((bf16[128,4096]{1,0:T(8,128)(2,1)S(1)}, bf16[128,4096]{1,0:T(8,128)(2,1)}, u32[]{:S(2)}, u32[]{:S(2)}) %collective-permute-start.5) | collective-permute-done | bytes 1048608 | tf_op jit(solution)/shard_map/ppermute | solution.py:231
  123.1 2.3 constant_dynamic-update-slice_fusion.8
  125.4 2.3 constant_dynamic-update-slice_fusion.7
  127.7 41.6 %collective-permute-done.7 = bf16[128,4096]{1,0:T(8,128)(2,1)} collective-permute-done((bf16[128,4096]{1,0:T(8,128)(2,1)S(1)}, bf16[128,4096]{1,0:T(8,128)(2,1)}, u32[]{:S(2)}, u32[]{:S(2)}) %collective-permute-start.7) | collective-permute-done | bytes 1048608 | tf_op jit(solution)/shard_map/ppermute | solution.py:231
  169.3 2.3 constant_dynamic-update-slice_fusion.6
  171.6 1.1 constant_dynamic-update-slice_fusion.5
  172.6 1.1 constant_dynamic-update-slice_fusion.4
  173.9 17.8 %all-gather.6.cloned.1.call-done = bf16[4096,768]{1,0:T(8,128)(2,1)} async-done(((bf16[1024,768]{1,0:T(8,128)(2,1)}), bf16[4096,768]{1,0:T(8,128)(2,1)}) %all-gather.6.cloned.1.call-update) | async-done | bytes 6291472 | tf_op jit(solution)/shard_map/all_gather | solution.py:273
  191.7 6.4 %fusion.6 = f32[1024,256]{0,1:T(8,128)S(1)} fusion(bf16[1024,4096]{1,0:T(8,128)(2,1)} %constant_dynamic-update-slice_fusion.4, bf16[4096,768]{1,0:T(8,128)(2,1)} %all-gather.6.cloned.1.call-done), kind=kOutput, calls=%fused_computation.14 | convolution fusion | flops 2147483648 | bytes 11534336 | tf_op jit(solution)/shard_map/dot_general | solution.py:280
  198.1 1.2 fusion.15
  199.4 1.1 copy.53
  200.8 3.1 multiply_cosine_fusion
  203.9 8.6 %fusion = f32[1024,512]{0,1:T(8,128)S(1)} fusion(bf16[1024,4096]{1,0:T(8,128)(2,1)} %constant_dynamic-update-slice_fusion.4, bf16[4096,768]{1,0:T(8,128)(2,1)} %all-gather.6.cloned.1.call-done), kind=kOutput, calls=%fused_computation.1 | convolution fusion | flops 4294967296 | bytes 14680064 | tf_op jit(solution)/shard_map/dot_general | solution.py:291
  212.5 1.2 fusion.26
  213.6 1.9 copy.60
  215.5 1.7 copy.61
  217.5 2.6 subtract_convert_fusion
  220.1 1.4 pad_maximum_fusion.1
  221.5 1.2 copy.71
  222.7 57.5 %all-gather.12.cloned.1.call-done = bf16[4160,256]{1,0:T(8,128)(2,1)} async-done(((bf16[1040,256]{1,0:T(8,128)(2,1)}), bf16[4160,256]{1,0:T(8,128)(2,1)}) %all-gather.12.cloned.1.call-update) | async-done | bytes 2129936 | tf_op jit(solution)/shard_map/all_gather | solution.py:285
  280.2 1.8 slice.136
  282.0 0.8 slice_bitcast_fusion.1
  282.8 1.8 convert_reduce_fusion
  284.6 5.2 %collective-permute-done.2 = bf16[4096,128]{1,0:T(8,128)(2,1)S(1)} collective-permute-done((bf16[4096,128]{1,0:T(8,128)(2,1)}, bf16[4096,128]{1,0:T(8,128)(2,1)S(1)}, u32[]{:S(2)}, u32[]{:S(2)}) %collective-permute-start.2) | collective-permute-done | bytes 1048608 | tf_op jit(solution)/shard_map/ppermute | solution.py:231
  289.8 1.0 copy-done.8
  291.3 5.5 %shard_map.73 = bf16[512,512]{1,0:T(8,128)(2,1)} custom-call(s32[2]{0:T(128)S(1)} %get-tuple-element.49.lo_ref, s32[2]{0:T(128)S(1)} %get-tuple-element.47.mid_ref, s32[2]{0:T(128)S(1)} %get-tuple-element.48.diag_ref, s32[2]{0:T(128)S(1)} %get-tuple-element.66.end_ref, s32[1]{0:T(128)} %bitcast.14.first_ref, bf16[512,512]{1,0:T(8,128)(2,1)S(1)} %get-tuple-element.58.q_ref, ...), custom_call_target="tpu_custom_call" | custom-call | flops 17179869184 | bytes 67108864 | tf_op jit(solution)/shard_map/pallas_call | solution.py:217
  297.1 7.7 %shard_map.74 = bf16[512,512]{1,0:T(8,128)(2,1)} custom-call(s32[2]{0:T(128)S(1)} %get-tuple-element.52.lo_ref, s32[2]{0:T(128)S(1)} %get-tuple-element.50.mid_ref, s32[2]{0:T(128)S(1)} %get-tuple-element.51.diag_ref, s32[2]{0:T(128)S(1)} %get-tuple-element.65.end_ref, s32[1]{0:T(128)} %bitcast.16.first_ref, bf16[512,512]{1,0:T(8,128)(2,1)S(1)} %get-tuple-element.42.q_ref, ...), custom_call_target="tpu_custom_call" | custom-call | flops 17179869184 | bytes 67108864 | tf_op jit(solution)/shard_map/pallas_call | solution.py:217
  304.9 2.3 broadcast_in_dim.13
  307.2 1.1 constant_dynamic-update-slice_fusion.3
  308.3 1.1 constant_dynamic-update-slice_fusion.2
  309.5 1.1 constant_dynamic-update-slice_fusion.1
  310.6 2.3 constant_dynamic-update-slice_fusion
  312.9 39.0 %all-gather.8.cloned.1.call-done = bf16[512,4096]{1,0:T(8,128)(2,1)} async-done(((bf16[512,512]{1,0:T(8,128)(2,1)}), bf16[512,4096]{1,0:T(8,128)(2,1)}) %all-gather.8.cloned.1.call-update) | async-done | bytes 4194320 | tf_op jit(solution)/shard_map/all_gather | solution.py:301
  351.9 5.8 %convolution_convert_fusion.1 = bf16[512,512]{1,0:T(8,128)(2,1)S(1)} fusion(bf16[512,4096]{1,0:T(8,128)(2,1)} %all-gather.8.cloned.1.call-done, bf16[4096,512]{1,0:T(8,128)(2,1)} %constant_dynamic-update-slice_fusion), kind=kOutput, calls=%fused_computation.17 | convolution fusion | flops 2147745792 | bytes 8912896 | tf_op jit(solution)/shard_map/dot_general | solution.py:306
  357.7 33.4 %all-gather.10.cloned.1.call-done = bf16[512,4096]{1,0:T(8,128)(2,1)} async-done(((bf16[512,512]{1,0:T(8,128)(2,1)}), bf16[512,4096]{1,0:T(8,128)(2,1)}) %all-gather.10.cloned.1.call-update) | async-done | bytes 4194320 | tf_op jit(solution)/shard_map/all_gather | solution.py:303
  391.1 5.8 %convolution_convert_fusion = bf16[512,512]{1,0:T(8,128)(2,1)S(1)} fusion(bf16[512,4096]{1,0:T(8,128)(2,1)} %all-gather.10.cloned.1.call-done, bf16[4096,512]{1,0:T(8,128)(2,1)} %constant_dynamic-update-slice_fusion), kind=kOutput, calls=%fused_computation.16 | convolution fusion | flops 2147745792 | bytes 8912896 | tf_op jit(solution)/shard_map/dot_general | solution.py:307
  397.0 17.9 %all_to_all.26 = bf16[8,128,512]{2,1,0:T(8,128)(2,1)S(1)} all-to-all(bf16[8,128,512]{2,1,0:T(8,128)(2,1)S(1)} %bitcast.62), channel_id=1, replica_groups=mesh['grp'=1,'seq'=16,'head'=1,'srv'=2] {'seq':(4)4,'srv'}, dimensions={0} | all-to-all | bytes 2097152 | tf_op jit(solution)/shard_map/all_to_all | solution.py:309
  415.2 1.7 reshape.240
  416.9 2.8 copy.58
  419.7 2.2 fusion.5
  (69 shorter events, 2.8 us)
Async XLA Ops:
  6.5 7.8 %copy-start = (bf16[128,4096]{1,0:T(8,128)(2,1)S(1)}, bf16[128,4096]{1,0:T(8,128)(2,1)}, u32[]{:S(2)}) copy-start(bf16[128,4096]{1,0:T(8,128)(2,1)} %param.9) | copy-start | bytes 3145732
  6.5 7.8 %copy-start.11 = (f32[4096]{0:T(1024)S(1)}, f32[4096]{0:T(1024)}, u32[]{:S(2)}) copy-start(f32[4096]{0:T(1024)} %param.10) | copy-start | bytes 49156
  12.6 3.2 copy-start.4
  12.6 3.2 copy-start.10
  19.0 56.4 %copy-start.2 = (bf16[128,4096]{1,0:T(8,128)(2,1)S(1)}, bf16[128,4096]{1,0:T(8,128)(2,1)}, u32[]{:S(2)}) copy-start(bf16[128,4096]{1,0:T(8,128)(2,1)} %fusion.4) | copy-start | bytes 3145732
  19.0 55.0 %all-to-all-start = ((bf16[144,8,768]{2,0,1:T(8,128)(2,1)}), bf16[144,8,768]{2,0,1:T(8,128)(2,1)S(1)}, u32[]{:S(2)}, u32[]{:S(2)}) async-start(bf16[144,8,768]{2,0,1:T(8,128)(2,1)} %copy.50), calls=%async_computation | async-start | bytes 3538944 | tf_op jit(solution)/shard_map/all_to_all | solution.py:266
  24.3 167.4 %all-gather.6.cloned.1.call-start = ((), (), s32[]{:S(2)}) async-start(), calls=%async_computation.2 | async-start | bytes 7864320 | tf_op jit(solution)/shard_map/all_gather | solution.py:273
  24.3 28.1 %collective-permute-start = (bf16[4096,128]{1,0:T(8,128)(2,1)}, bf16[4096,128]{1,0:T(8,128)(2,1)S(1)}, u32[]{:S(2)}, u32[]{:S(2)}) collective-permute-start(bf16[4096,128]{1,0:T(8,128)(2,1)} %param.14), channel_id=1, source_target_pairs={{0,8},{8,16},{16,24},{24,0},{1,9},{9,17},{17,25},{25,1},{2,10},{10... | collective-permute-start | bytes 3145736 | tf_op jit(solution)/shard_map/ppermute | solution.py:231
  25.9 48.0 %collective-permute-start.1 = (bf16[4096,128]{1,0:T(8,128)(2,1)}, bf16[4096,128]{1,0:T(8,128)(2,1)}, u32[]{:S(2)}, u32[]{:S(2)}) collective-permute-start(bf16[4096,128]{1,0:T(8,128)(2,1)} %param.14), channel_id=1, source_target_pairs={{0,24},{8,0},{16,8},{24,16},{1,25},{9,1},{17,9},{25,17},{2,26},{10... | collective-permute-start | bytes 3145736 | tf_op jit(solution)/shard_map/ppermute | solution.py:231
  52.4 1.0 copy-start.6
  75.3 204.9 %all-gather.12.cloned.1.call-start = ((), (), s32[]{:S(2)}) async-start(), calls=%async_computation.5 | async-start | bytes 2662400 | tf_op jit(solution)/shard_map/all_gather | solution.py:285
  75.3 9.1 %collective-permute-start.3 = (bf16[128,4096]{1,0:T(8,128)(2,1)S(1)}, bf16[128,4096]{1,0:T(8,128)(2,1)}, u32[]{:S(2)}, u32[]{:S(2)}) collective-permute-start(bf16[128,4096]{1,0:T(8,128)(2,1)S(1)} %copy-done.2), channel_id=1, source_target_pairs={{0,1},{1,0},{2,3},{3,2},{4,5},{5,4},{6,7},{7,6},{8,9},{9,8},{10,11... | collective-permute-start | bytes 3145736 | tf_op jit(solution)/shard_map/ppermute | solution.py:231
  75.4 26.1 %collective-permute-start.4 = (bf16[128,4096]{1,0:T(8,128)(2,1)S(1)}, bf16[128,4096]{1,0:T(8,128)(2,1)}, u32[]{:S(2)}, u32[]{:S(2)}) collective-permute-start(bf16[128,4096]{1,0:T(8,128)(2,1)S(1)} %copy-done.2), channel_id=1, source_target_pairs={{0,2},{1,3},{2,0},{3,1},{4,6},{5,7},{6,4},{7,5},{8,10},{9,11},{10,... | collective-permute-start | bytes 3145736 | tf_op jit(solution)/shard_map/ppermute | solution.py:231
  77.1 46.0 %collective-permute-start.5 = (bf16[128,4096]{1,0:T(8,128)(2,1)S(1)}, bf16[128,4096]{1,0:T(8,128)(2,1)}, u32[]{:S(2)}, u32[]{:S(2)}) collective-permute-start(bf16[128,4096]{1,0:T(8,128)(2,1)S(1)} %copy-done.2), channel_id=1, source_target_pairs={{0,3},{1,2},{2,1},{3,0},{4,7},{5,6},{6,5},{7,4},{8,11},{9,10},{10,... | collective-permute-start | bytes 3145736 | tf_op jit(solution)/shard_map/ppermute | solution.py:231
  77.3 48.1 %collective-permute-start.6 = (bf16[128,4096]{1,0:T(8,128)(2,1)S(1)}, bf16[128,4096]{1,0:T(8,128)(2,1)}, u32[]{:S(2)}, u32[]{:S(2)}) collective-permute-start(bf16[128,4096]{1,0:T(8,128)(2,1)S(1)} %copy-done.2), channel_id=1, source_target_pairs={{0,4},{1,5},{2,6},{3,7},{4,0},{5,1},{6,2},{7,3},{8,12},{9,13},{10,... | collective-permute-start | bytes 3145736 | tf_op jit(solution)/shard_map/ppermute | solution.py:231
  78.9 90.3 %collective-permute-start.7 = (bf16[128,4096]{1,0:T(8,128)(2,1)S(1)}, bf16[128,4096]{1,0:T(8,128)(2,1)}, u32[]{:S(2)}, u32[]{:S(2)}) collective-permute-start(bf16[128,4096]{1,0:T(8,128)(2,1)S(1)} %copy-done.2), channel_id=1, source_target_pairs={{0,5},{1,4},{2,7},{3,6},{4,1},{5,0},{6,3},{7,2},{8,13},{9,12},{10,... | collective-permute-start | bytes 3145736 | tf_op jit(solution)/shard_map/ppermute | solution.py:231
  84.4 87.2 %collective-permute-start.8 = (bf16[128,4096]{1,0:T(8,128)(2,1)S(1)}, bf16[128,4096]{1,0:T(8,128)(2,1)S(1)}, u32[]{:S(2)}, u32[]{:S(2)}) collective-permute-start(bf16[128,4096]{1,0:T(8,128)(2,1)S(1)} %copy-done.2), channel_id=1, source_target_pairs={{0,6},{1,7},{2,4},{3,5},{4,2},{5,3},{6,0},{7,1},{8,14},{9,15},{10,... | collective-permute-start | bytes 3145736 | tf_op jit(solution)/shard_map/ppermute | solution.py:231
  101.5 71.1 %collective-permute-start.9 = (bf16[128,4096]{1,0:T(8,128)(2,1)S(1)}, bf16[128,4096]{1,0:T(8,128)(2,1)S(1)}, u32[]{:S(2)}, u32[]{:S(2)}) collective-permute-start(bf16[128,4096]{1,0:T(8,128)(2,1)S(1)} %copy-done.2), channel_id=1, source_target_pairs={{0,7},{1,6},{2,5},{3,4},{4,3},{5,2},{6,1},{7,0},{8,15},{9,14},{10,... | collective-permute-start | bytes 3145736 | tf_op jit(solution)/shard_map/ppermute | solution.py:231
  200.5 151.4 %all-gather.8.cloned.1.call-start = ((), (), s32[]{:S(2)}) async-start(), calls=%async_computation.3 | async-start | bytes 4718592 | tf_op jit(solution)/shard_map/all_gather | solution.py:301
  217.2 72.5 %collective-permute-start.2 = (bf16[4096,128]{1,0:T(8,128)(2,1)}, bf16[4096,128]{1,0:T(8,128)(2,1)S(1)}, u32[]{:S(2)}, u32[]{:S(2)}) collective-permute-start(bf16[4096,128]{1,0:T(8,128)(2,1)} %param.14), channel_id=1, source_target_pairs={{0,16},{8,24},{16,0},{24,8},{1,17},{9,25},{17,1},{25,9},{2,18},{10... | collective-permute-start | bytes 3145736 | tf_op jit(solution)/shard_map/ppermute | solution.py:231
  280.2 10.6 %copy-start.3 = (bf16[128,8,4,128]{3,1,2,0:T(8,128)(2,1)S(1)}, bf16[128,8,4,128]{3,1,2,0:T(8,128)(2,1)}, u32[]{:S(2)}) copy-start(bf16[128,8,4,128]{3,1,2,0:T(8,128)(2,1)} %copy.71) | copy-start | bytes 3145732
  289.8 1.0 copy-start.8
  296.9 94.2 %all-gather.10.cloned.1.call-start = ((), (), s32[]{:S(2)}) async-start(), calls=%async_computation.4 | async-start | bytes 4718592 | tf_op jit(solution)/shard_map/all_gather | solution.py:303
  304.8 2.5 copy-start.5
  304.8 3.5 copy-start.7
  304.9 4.6 %copy-start.9 = (bf16[4096,128]{1,0:T(8,128)(2,1)S(1)}, bf16[4096,128]{1,0:T(8,128)(2,1)}, u32[]{:S(2)}) copy-start(bf16[4096,128]{1,0:T(8,128)(2,1)} %copy-done.8) | copy-start | bytes 3145732
  415.2 4.5 %copy-start.1 = (bf16[128,4096]{1,0:T(8,128)(2,1)S(1)}, bf16[128,4096]{1,0:T(8,128)(2,1)}, u32[]{:S(2)}) copy-start(bf16[128,4096]{1,0:T(8,128)(2,1)} %param.9) | copy-start | bytes 3145732
Sparse Core Ops, SparseCore 0:
  75.4 116.2 all-gather.5
  200.6 79.4 all-gather.11
  297.0 54.8 all-gather.7
  353.6 37.4 all-gather.9
